TPU v7x, 256 devices: a whole 4x4x8 slice. The times are simulated.
256 devices in a mesh: sector: 16 (over y_lo, z), band: 16 (over y_hi, x, core).
Axes of the slice: x: 4, y: 4 (y_hi: 2, y_lo: 2; y = y_hi * 2 + y_lo), z: 8, core: 2. Of those that a mesh axis runs over, the one named last changes fastest.
Arguments:
- gas_density: bfloat16 [6144, 8192], P('band', 'sector'), may hold values from 0.29882812 to 3
- green_radial: bfloat16 [5, 6144, 1152], P(None, 'band'), may hold values from -0.1875 to 0.1875
- green_azimuth: bfloat16 [5, 512, 512], replicated, may hold values from -0.25 to 0.25
- dust_density: float32 [6144, 8192], P('band', 'sector'), may hold values from 0.2 to 2
- dust_radial_velocity: float32 [6144, 8192], P('band', 'sector'), may hold values from -1.5 to 1.5
- dust_azimuth_velocity: float32 [6144, 8192], P('band', 'sector'), may hold values from -1.5 to 1.5
- coupling: bfloat16 [6144, 8192], P('band', 'sector'), may hold values from 0.019897461 to 0.5
Outputs:
- potential: float32 [6144, 8192], P('band', 'sector')
- density_next: float32 [6144, 8192], P('band', 'sector')
- radial_next: float32 [6144, 8192], P('band', 'sector')
- azimuth_next: float32 [6144, 8192], P('band', 'sector')
All inputs are finite; a program needn't handle non-finite values.
Results may differ from a plain program's by a relative error of at most 0.0028.
Values may be sent and summed in bfloat16 or wider, within the bound.
A program may use at most 128 MiB of HBM per device.

v0:
```python
import jax
import jax.numpy as jnp
from jax import lax
from jax.sharding import PartitionSpec as P

diffusion = 0.1
gravity = 0.1
kepler = 0.6


def padded(block, sides, width, periodic):
    for axis, dim in sides:
        count = lax.axis_size(axis)
        forward = [(i, i + 1) for i in range(count - 1)]
        if periodic:
            forward.append((count - 1, 0))
        backward = [(target, source) for source, target in forward]
        low = lax.ppermute(
            lax.slice_in_dim(block, block.shape[dim] - width, None, axis=dim), axis, forward
        )
        high = lax.ppermute(lax.slice_in_dim(block, 0, width, axis=dim), axis, backward)
        block = jnp.concatenate([low, block, high], axis=dim)
    return block


def passed_along(value, axis, steps):
    count = lax.axis_size(axis)
    pairs = [(source, (source + steps) % count) for source in range(count)]
    return lax.ppermute(value, axis, pairs)


def advance_dust(
    centre,
    upper_rows,
    lower_rows,
    east_side,
    west_side,
    potential_up,
    potential_down,
    potential_east,
    potential_west,
    coupling_rate,
    inv_radius,
):
    density = centre[0]
    radial = centre[1]
    azimuth = centre[2]
    laplace = upper_rows + lower_rows + east_side + west_side - 4.0 * centre
    flux_up = upper_rows[0] * upper_rows[1]
    flux_down = lower_rows[0] * lower_rows[1]
    flux_east = east_side[0] * east_side[2]
    flux_west = west_side[0] * west_side[2]
    gas_speed = kepler * jnp.sqrt(inv_radius)
    density_next = (
        density
        - 0.5 * (flux_up - flux_down)
        - 0.5 * inv_radius * (flux_east - flux_west)
        + diffusion * laplace[0]
    )
    radial_next = (
        radial
        - 0.5 * radial * (upper_rows[1] - lower_rows[1])
        - 0.5 * inv_radius * azimuth * (east_side[1] - west_side[1])
        - 0.5 * gravity * (potential_up - potential_down)
        - coupling_rate * radial
        + diffusion * laplace[1]
    )
    azimuth_next = (
        azimuth
        - 0.5 * radial * (upper_rows[2] - lower_rows[2])
        - 0.5 * inv_radius * azimuth * (east_side[2] - west_side[2])
        - 0.5 * gravity * inv_radius * (potential_east - potential_west)
        - coupling_rate * (azimuth - gas_speed)
        + diffusion * laplace[2]
    )
    return (density_next, radial_next, azimuth_next)


def radial_part(extended, offset, green_radial):
    return jnp.dot(green_radial[offset + 2], extended, preferred_element_type=jnp.float32).astype(
        jnp.bfloat16
    )


def green_term(extended, offset, green_radial, green_azimuth):
    radial = radial_part(extended, offset, green_radial)
    return jnp.dot(radial, green_azimuth[offset + 2], preferred_element_type=jnp.float32)


def body(
    gas_density,
    green_radial,
    green_azimuth,
    dust_density,
    dust_radial_velocity,
    dust_azimuth_velocity,
    coupling,
):
    rows = dust_density.shape[0]
    fields = jnp.stack([dust_density, dust_radial_velocity, dust_azimuth_velocity])
    extended = padded(gas_density, (("band", 0),), rows, False)
    potential = green_term(extended, 0, green_radial, green_azimuth)
    rising = extended
    falling = extended
    for offset in (1, 2):
        rising = passed_along(rising, "sector", 1)
        potential = potential + green_term(rising, offset, green_radial, green_azimuth)
        falling = passed_along(falling, "sector", -1)
        potential = potential + green_term(falling, -offset, green_radial, green_azimuth)
    joined = jnp.concatenate([fields, potential[None]], axis=0)
    joined_rows = padded(joined, (("band", 1),), 1, False)
    joined_cols = padded(joined, (("sector", 2),), 1, True)
    band_rims = joined_rows[:3]
    sector_rims = joined_cols[:3]
    potential_rows = joined_rows[3]
    potential_cols = joined_cols[3]
    row_index = lax.axis_index("band") * rows + jnp.arange(rows, dtype=jnp.int32)
    total_rows = rows * lax.axis_size("band")
    inv_radius = (1.0 / (1.0 + 3.0 * (row_index.astype(jnp.float32) + 0.5) / total_rows))[:, None]
    density_next, radial_next, azimuth_next = advance_dust(
        fields,
        band_rims[:, 2:],
        band_rims[:, :-2],
        sector_rims[:, :, 2:],
        sector_rims[:, :, :-2],
        potential_rows[2:],
        potential_rows[:-2],
        potential_cols[:, 2:],
        potential_cols[:, :-2],
        coupling.astype(jnp.float32),
        inv_radius,
    )
    return (potential, density_next, radial_next, azimuth_next)


def solution(mesh):
    return jax.shard_map(
        body,
        mesh=mesh,
        in_specs=(
            P("band", "sector"),
            P(None, "band", None),
            P(),
            P("band", "sector"),
            P("band", "sector"),
            P("band", "sector"),
            P("band", "sector"),
        ),
        out_specs=(
            P("band", "sector"),
            P("band", "sector"),
            P("band", "sector"),
            P("band", "sector"),
        ),
        check_vma=False,
    )
```

profile of v0, /device:TPU:1, one launch (start us, length us, event | category | flops | bytes accessed | tf_op | source)
XLA Modules:
  0.0 110.9 jit_solution(50707923501142072)
XLA Ops:
  0.6 4.5 %collective-permute-start = (bf16[384,512]{1,0:T(8,128)(2,1)}, bf16[384,512]{1,0:T(8,128)(2,1)S(1)}, u32[]{:S(2)}, u32[]{:S(2)}) collective-permute-start(bf16[384,512]{1,0:T(8,128)(2,1)} %param.7), channel_id=1, source_target_pairs={{0,1},{1,2},{2,3},{3,4},{4,5},{5,6},{6,7},{7,8},{8,9},{9,10},{10,1... | collective-permute-start | bytes 1179656 | tf_op jit(solution)/shard_map/ppermute | solution.py:18
  5.1 2.0 %collective-permute-start.1 = (bf16[384,512]{1,0:T(8,128)(2,1)}, bf16[384,512]{1,0:T(8,128)(2,1)S(1)}, u32[]{:S(2)}, u32[]{:S(2)}) collective-permute-start(bf16[384,512]{1,0:T(8,128)(2,1)} %param.7), channel_id=1, source_target_pairs={{1,0},{2,1},{3,2},{4,3},{5,4},{6,5},{7,6},{8,7},{9,8},{10,9},{11,1... | collective-permute-start | bytes 1179656 | tf_op jit(solution)/shard_map/ppermute | solution.py:21
  7.1 3.1 %collective-permute-done = bf16[384,512]{1,0:T(8,128)(2,1)S(1)} collective-permute-done((bf16[384,512]{1,0:T(8,128)(2,1)}, bf16[384,512]{1,0:T(8,128)(2,1)S(1)}, u32[]{:S(2)}, u32[]{:S(2)}) %collective-permute-start) | collective-permute-done | bytes 393248 | tf_op jit(solution)/shard_map/ppermute | solution.py:18
  11.2 3.6 %collective-permute-done.1 = bf16[384,512]{1,0:T(8,128)(2,1)S(1)} collective-permute-done((bf16[384,512]{1,0:T(8,128)(2,1)}, bf16[384,512]{1,0:T(8,128)(2,1)S(1)}, u32[]{:S(2)}, u32[]{:S(2)}) %collective-permute-start.1) | collective-permute-done | bytes 393248 | tf_op jit(solution)/shard_map/ppermute | solution.py:21
  14.9 1.7 %collective-permute-start.2 = (bf16[1152,512]{1,0:T(8,128)(2,1)S(1)}, bf16[1152,512]{1,0:T(8,128)(2,1)S(1)}, u32[]{:S(2)}, u32[]{:S(2)}) collective-permute-start(bf16[1152,512]{1,0:T(8,128)(2,1)S(1)} %constant_dynamic-update-slice_fusion), channel_id=1, source_target_pairs={{0,16},{16,32},{32,48},{48,64},{64,80},{80,96},{96,112},{112,128},... | collective-permute-start | bytes 3538952 | tf_op jit(solution)/shard_map/ppermute | solution.py:29
  16.6 5.0 %collective-permute-start.3 = (bf16[1152,512]{1,0:T(8,128)(2,1)S(1)}, bf16[1152,512]{1,0:T(8,128)(2,1)}, u32[]{:S(2)}, u32[]{:S(2)}) collective-permute-start(bf16[1152,512]{1,0:T(8,128)(2,1)S(1)} %constant_dynamic-update-slice_fusion), channel_id=1, source_target_pairs={{0,240},{16,0},{32,16},{48,32},{64,48},{80,64},{96,80},{112,96},{1... | collective-permute-start | bytes 3538952 | tf_op jit(solution)/shard_map/ppermute | solution.py:29
  21.6 20.9 %collective-permute-done.2 = bf16[1152,512]{1,0:T(8,128)(2,1)S(1)} collective-permute-done((bf16[1152,512]{1,0:T(8,128)(2,1)S(1)}, bf16[1152,512]{1,0:T(8,128)(2,1)S(1)}, u32[]{:S(2)}, u32[]{:S(2)}) %collective-permute-start.2) | collective-permute-done | bytes 1179680 | tf_op jit(solution)/shard_map/ppermute | solution.py:29
  42.6 3.9 %collective-permute-start.5 = (bf16[1152,512]{1,0:T(8,128)(2,1)}, bf16[1152,512]{1,0:T(8,128)(2,1)}, u32[]{:S(2)}, u32[]{:S(2)}) collective-permute-start(bf16[1152,512]{1,0:T(8,128)(2,1)} %collective-permute-done.3), channel_id=1, source_target_pairs={{0,240},{16,0},{32,16},{48,32},{64,48},{80,64},{96,80},{112,96},{1... | collective-permute-start | bytes 3538952 | tf_op jit(solution)/shard_map/ppermute | solution.py:29
  46.5 2.5 %fusion.1 = f32[384,512]{1,0:T(8,128)S(1)} fusion(bf16[1152,512]{1,0:T(8,128)(2,1)S(1)} %constant_dynamic-update-slice_fusion, bf16[5,384,1152]{2,1,0:T(8,128)(2,1)} %param.8, bf16[5,512,512]{2,1,0:T(8,128)(2,1)} %param.9), kind=kOutput, calls=%fused_computation.18 | convolution fusion | flops 654508032 | bytes 3375104 | tf_op jit(solution)/shard_map/dot_general | solution.py:87
  49.0 2.5 %convolution_add_fusion.3 = f32[384,512]{1,0:T(8,128)S(1)} fusion(f32[384,512]{1,0:T(8,128)S(1)} %fusion.1, bf16[1152,512]{1,0:T(8,128)(2,1)S(1)} %collective-permute-done.2, bf16[5,384,1152]{2,1,0:T(8,128)(2,1)} %param.8, bf16[5,512,512]{2,1,0:T(8,128)(2,1)} %param.9), kind=kOutput, calls=%fused_computation.12 | convolution fusion | flops 654704640 | bytes 4161536 | tf_op jit(solution)/shard_map/dot_general | solution.py:87
  51.5 2.9 %convolution_add_fusion.2 = f32[384,512]{1,0:T(8,128)S(1)} fusion(f32[384,512]{1,0:T(8,128)S(1)} %convolution_add_fusion.3, bf16[1152,512]{1,0:T(8,128)(2,1)} %collective-permute-done.3, bf16[5,384,1152]{2,1,0:T(8,128)(2,1)} %param.8, bf16[5,512,512]{2,1,0:T(8,128)(2,1)} %param.9), kind=kOutput, calls=%fused_computation.11 | convolution fusion | flops 654704640 | bytes 4161536 | tf_op jit(solution)/shard_map/dot_general | solution.py:87
  54.4 13.1 %collective-permute-done.4 = bf16[1152,512]{1,0:T(8,128)(2,1)} collective-permute-done((bf16[1152,512]{1,0:T(8,128)(2,1)S(1)}, bf16[1152,512]{1,0:T(8,128)(2,1)}, u32[]{:S(2)}, u32[]{:S(2)}) %collective-permute-start.4) | collective-permute-done | bytes 1179680 | tf_op jit(solution)/shard_map/ppermute | solution.py:29
  67.5 3.7 %convolution_add_fusion.1 = f32[384,512]{1,0:T(8,128)} fusion(f32[384,512]{1,0:T(8,128)S(1)} %convolution_add_fusion.2, bf16[1152,512]{1,0:T(8,128)(2,1)} %collective-permute-done.4, bf16[5,384,1152]{2,1,0:T(8,128)(2,1)} %param.8, bf16[5,512,512]{2,1,0:T(8,128)(2,1)} %param.9), kind=kOutput, calls=%fused_computation.10 | convolution fusion | flops 654704640 | bytes 4161536 | tf_op jit(solution)/shard_map/dot_general | solution.py:87
  71.2 3.3 %convolution_add_fusion = f32[384,512]{1,0:T(8,128)S(1)} fusion(f32[384,512]{1,0:T(8,128)} %convolution_add_fusion.1, bf16[1152,512]{1,0:T(8,128)(2,1)} %collective-permute-done.5, bf16[5,384,1152]{2,1,0:T(8,128)(2,1)} %param.8, bf16[5,512,512]{2,1,0:T(8,128)(2,1)} %param.9), kind=kOutput, calls=%fused_computation.9 | convolution fusion | flops 654704640 | bytes 4161536 | tf_op jit(solution)/shard_map/dot_general | solution.py:87
  74.5 1.4 %pad_maximum_fusion.12 = (f32[4,384,1]{2,1,0:T(8,128)}, f32[4,384,1]{2,1,0:T(8,128)}) fusion(f32[1,384,512]{2,1,0:T(8,128)S(1)} %bitcast.133, f32[1,384,512]{2,1,0:T(8,128)S(1)} %bitcast.106, f32[1,384,512]{2,1,0:T(8,128)S(1)} %bitcast.115, f32[1,384,512]{2,1,0:T(8,128)S(1)} %bitcast.124), kind=kLoop, calls=%fused_computation.75 | loop fusion | flops 9216 | bytes 3158016 | tf_op jit(solution)/shard_map/slice | solution.py:21
  76.0 1.4 %copy.11 = f32[4,384,1]{1,0,2:T(4,128)S(1)} copy(f32[4,384,1]{2,1,0:T(8,128)} %get-tuple-element.10) | data formatting | bytes 12288 | tf_op jit(solution)/shard_map/slice | solution.py:21
  77.3 1.8 %collective-permute-start.8 = (f32[4,384,1]{1,0,2:T(4,128)S(1)}, f32[4,384,1]{1,0,2:T(4,128)S(1)}, u32[]{:S(2)}, u32[]{:S(2)}) collective-permute-start(f32[4,384,1]{1,0,2:T(4,128)S(1)} %copy.11), channel_id=1, source_target_pairs={{16,0},{32,16},{48,32},{64,48},{80,64},{96,80},{112,96},{128,112},... | collective-permute-start | bytes 18440 | tf_op jit(solution)/shard_map/ppermute | solution.py:21
  79.1 1.4 %copy.13 = f32[4,384,1]{1,0,2:T(4,128)S(1)} copy(f32[4,384,1]{2,1,0:T(8,128)} %get-tuple-element.11) | data formatting | bytes 12288 | tf_op jit(solution)/shard_map/slice | solution.py:19
  80.6 1.9 %collective-permute-start.6 = (f32[4,1,512]{2,1,0:T(1,128)S(1)}, f32[4,1,512]{2,1,0:T(1,128)S(1)}, u32[]{:S(2)}, u32[]{:S(2)}) collective-permute-start(f32[4,1,512]{2,1,0:T(1,128)S(1)} %get-tuple-element.6), channel_id=1, source_target_pairs={{1,0},{2,1},{3,2},{4,3},{5,4},{6,5},{7,6},{8,7},{9,8},{10,9},{11,1... | collective-permute-start | bytes 24584 | tf_op jit(solution)/shard_map/ppermute | solution.py:21
  82.5 13.0 %collective-permute-start.7 = (f32[4,1,512]{2,1,0:T(1,128)S(1)}, f32[4,1,512]{2,1,0:T(1,128)S(1)}, u32[]{:S(2)}, u32[]{:S(2)}) collective-permute-start(f32[4,1,512]{2,1,0:T(1,128)S(1)} %get-tuple-element.7), channel_id=1, source_target_pairs={{0,1},{1,2},{2,3},{3,4},{4,5},{5,6},{6,7},{7,8},{8,9},{9,10},{10,1... | collective-permute-start | bytes 24584 | tf_op jit(solution)/shard_map/ppermute | solution.py:18
  97.9 3.7 %pad_maximum_fusion = (f32[4,384,513]{2,1,0:T(8,128)S(1)}, f32[4,384,513]{2,1,0:T(8,128)S(1)}) fusion(f32[4,384,1]{2,1,0:T(8,128)} %copy.12, f32[1,384,512]{2,1,0:T(8,128)S(1)} %bitcast.135, f32[1,384,512]{2,1,0:T(8,128)S(1)} %bitcast.108, f32[1,384,512]{2,1,0:T(8,128)S(1)} %bitcast.117, f32[1,384,512]{2,1,0:T(8,128)S(1)} %bitcast.126, f32[4,384,1]{2,1,0:T(8,128)} %copy.14), kind=kLoop, calls=%fused_computation | loop fusion | flops 6303744 | bytes 9461760 | tf_op jit(solution)/shard_map/concatenate | solution.py:22
  104.4 2.5 %fusion.42 = f32[384,512]{1,0:T(8,128)} fusion(f32[3,384,512]{2,1,0:T(8,128)S(1)} %fusion, f32[4,384,1]{2,1,0:T(8,128)S(1)} %copy-done.5, f32[1,384,512]{2,1,0:T(8,128)S(1)} %bitcast.138, f32[1,384,512]{2,1,0:T(8,128)S(1)} %bitcast.112, f32[1,384,512]{2,1,0:T(8,128)S(1)} %bitcast.121, f32[1,384,512]{2,1,0:T(8,128)S(1)} %bitcast.130, ...), kind=kLoop, calls=%fused_computation.63 | loop fusion | flops 5505024 | bytes 8664576 | tf_op jit(solution)/shard_map/add | solution.py:55
  107.0 1.9 %fusion.24 = f32[384,512]{1,0:T(8,128)} fusion(f32[384,512]{1,0:T(8,128)S(1)} %copy-done.1, bf16[384,512]{1,0:T(8,128)(2,1)S(1)} %copy-done.6, f32[3,384,512]{2,1,0:T(8,128)S(1)} %fusion, f32[4,385,512]{2,1,0:T(8,128)S(1)} %get-tuple-element.5, f32[4,385,512]{2,1,0:T(8,128)S(1)} %get-tuple-element.4, f32[4,384,1]{2,1,0:T(8,128)S(1)} %copy-done.5, ...), kind=kLoop, calls=%fused_computation.38 | loop fusion | flops 4718592 | bytes 9844224 | tf_op jit(solution)/shard_map/add | solution.py:61
  108.9 2.0 %fusion.26 = f32[384,512]{1,0:T(8,128)} fusion(bf16[384,512]{1,0:T(8,128)(2,1)S(1)} %copy-done.6, f32[3,384,512]{2,1,0:T(8,128)S(1)} %fusion, f32[384,514]{1,0:T(8,128)S(1)} %fusion.2, f32[384,512]{1,0:T(8,128)S(1)} %copy-done, f32[4,385,512]{2,1,0:T(8,128)S(1)} %get-tuple-element.5, f32[4,385,512]{2,1,0:T(8,128)S(1)} %get-tuple-element.4, ...), kind=kLoop, calls=%fused_computation.40 | loop fusion | flops 4915200 | bytes 9847296 | tf_op jit(solution)/shard_map/add | solution.py:69
  (33 shorter events, 6.3 us)
Async XLA Ops:
  0.6 9.5 %collective-permute-start = (bf16[384,512]{1,0:T(8,128)(2,1)}, bf16[384,512]{1,0:T(8,128)(2,1)S(1)}, u32[]{:S(2)}, u32[]{:S(2)}) collective-permute-start(bf16[384,512]{1,0:T(8,128)(2,1)} %param.7), channel_id=1, source_target_pairs={{0,1},{1,2},{2,3},{3,4},{4,5},{5,6},{6,7},{7,8},{8,9},{9,10},{10,1... | collective-permute-start | bytes 1179656 | tf_op jit(solution)/shard_map/ppermute | solution.py:18
  5.1 9.7 %collective-permute-start.1 = (bf16[384,512]{1,0:T(8,128)(2,1)}, bf16[384,512]{1,0:T(8,128)(2,1)S(1)}, u32[]{:S(2)}, u32[]{:S(2)}) collective-permute-start(bf16[384,512]{1,0:T(8,128)(2,1)} %param.7), channel_id=1, source_target_pairs={{1,0},{2,1},{3,2},{4,3},{5,4},{6,5},{7,6},{8,7},{9,8},{10,9},{11,1... | collective-permute-start | bytes 1179656 | tf_op jit(solution)/shard_map/ppermute | solution.py:21
  14.9 27.6 %collective-permute-start.2 = (bf16[1152,512]{1,0:T(8,128)(2,1)S(1)}, bf16[1152,512]{1,0:T(8,128)(2,1)S(1)}, u32[]{:S(2)}, u32[]{:S(2)}) collective-permute-start(bf16[1152,512]{1,0:T(8,128)(2,1)S(1)} %constant_dynamic-update-slice_fusion), channel_id=1, source_target_pairs={{0,16},{16,32},{32,48},{48,64},{64,80},{80,96},{96,112},{112,128},... | collective-permute-start | bytes 3538952 | tf_op jit(solution)/shard_map/ppermute | solution.py:29
  16.6 25.9 %collective-permute-start.3 = (bf16[1152,512]{1,0:T(8,128)(2,1)S(1)}, bf16[1152,512]{1,0:T(8,128)(2,1)}, u32[]{:S(2)}, u32[]{:S(2)}) collective-permute-start(bf16[1152,512]{1,0:T(8,128)(2,1)S(1)} %constant_dynamic-update-slice_fusion), channel_id=1, source_target_pairs={{0,240},{16,0},{32,16},{48,32},{64,48},{80,64},{96,80},{112,96},{1... | collective-permute-start | bytes 3538952 | tf_op jit(solution)/shard_map/ppermute | solution.py:29
  42.5 25.0 %collective-permute-start.4 = (bf16[1152,512]{1,0:T(8,128)(2,1)S(1)}, bf16[1152,512]{1,0:T(8,128)(2,1)}, u32[]{:S(2)}, u32[]{:S(2)}) collective-permute-start(bf16[1152,512]{1,0:T(8,128)(2,1)S(1)} %collective-permute-done.2), channel_id=1, source_target_pairs={{0,16},{16,32},{32,48},{48,64},{64,80},{80,96},{96,112},{112,128},... | collective-permute-start | bytes 3538952 | tf_op jit(solution)/shard_map/ppermute | solution.py:29
  42.6 28.7 %collective-permute-start.5 = (bf16[1152,512]{1,0:T(8,128)(2,1)}, bf16[1152,512]{1,0:T(8,128)(2,1)}, u32[]{:S(2)}, u32[]{:S(2)}) collective-permute-start(bf16[1152,512]{1,0:T(8,128)(2,1)} %collective-permute-done.3), channel_id=1, source_target_pairs={{0,240},{16,0},{32,16},{48,32},{64,48},{80,64},{96,80},{112,96},{1... | collective-permute-start | bytes 3538952 | tf_op jit(solution)/shard_map/ppermute | solution.py:29
  71.2 3.3 %copy-start = (f32[384,512]{1,0:T(8,128)S(1)}, f32[384,512]{1,0:T(8,128)}, u32[]{:S(2)}) copy-start(f32[384,512]{1,0:T(8,128)} %param.12) | copy-start | bytes 2359300
  71.2 3.3 %copy-start.1 = (f32[384,512]{1,0:T(8,128)S(1)}, f32[384,512]{1,0:T(8,128)}, u32[]{:S(2)}) copy-start(f32[384,512]{1,0:T(8,128)} %param.11) | copy-start | bytes 2359300
  71.2 3.3 %copy-start.2 = (f32[384,512]{1,0:T(8,128)S(1)}, f32[384,512]{1,0:T(8,128)}, u32[]{:S(2)}) copy-start(f32[384,512]{1,0:T(8,128)} %param.10) | copy-start | bytes 2359300
  74.5 34.4 %copy-start.3 = (f32[384,512]{1,0:T(8,128)}, f32[384,512]{1,0:T(8,128)S(1)}, u32[]{:S(2)}) copy-start(f32[384,512]{1,0:T(8,128)S(1)} %convolution_add_fusion) | copy-start | bytes 2359300
  77.3 18.2 %collective-permute-start.8 = (f32[4,384,1]{1,0,2:T(4,128)S(1)}, f32[4,384,1]{1,0,2:T(4,128)S(1)}, u32[]{:S(2)}, u32[]{:S(2)}) collective-permute-start(f32[4,384,1]{1,0,2:T(4,128)S(1)} %copy.11), channel_id=1, source_target_pairs={{16,0},{32,16},{48,32},{64,48},{80,64},{96,80},{112,96},{128,112},... | collective-permute-start | bytes 18440 | tf_op jit(solution)/shard_map/ppermute | solution.py:21
  80.5 16.2 %collective-permute-start.9 = (f32[4,384,1]{1,0,2:T(4,128)S(1)}, f32[4,384,1]{1,0,2:T(4,128)S(1)}, u32[]{:S(2)}, u32[]{:S(2)}) collective-permute-start(f32[4,384,1]{1,0,2:T(4,128)S(1)} %copy.13), channel_id=1, source_target_pairs={{0,16},{16,32},{32,48},{48,64},{64,80},{80,96},{96,112},{112,128},... | collective-permute-start | bytes 18440 | tf_op jit(solution)/shard_map/ppermute | solution.py:18
  80.6 21.5 %collective-permute-start.6 = (f32[4,1,512]{2,1,0:T(1,128)S(1)}, f32[4,1,512]{2,1,0:T(1,128)S(1)}, u32[]{:S(2)}, u32[]{:S(2)}) collective-permute-start(f32[4,1,512]{2,1,0:T(1,128)S(1)} %get-tuple-element.6), channel_id=1, source_target_pairs={{1,0},{2,1},{3,2},{4,3},{5,4},{6,5},{7,6},{8,7},{9,8},{10,9},{11,1... | collective-permute-start | bytes 24584 | tf_op jit(solution)/shard_map/ppermute | solution.py:21
  82.5 19.5 %collective-permute-start.7 = (f32[4,1,512]{2,1,0:T(1,128)S(1)}, f32[4,1,512]{2,1,0:T(1,128)S(1)}, u32[]{:S(2)}, u32[]{:S(2)}) collective-permute-start(f32[4,1,512]{2,1,0:T(1,128)S(1)} %get-tuple-element.7), channel_id=1, source_target_pairs={{0,1},{1,2},{2,3},{3,4},{4,5},{5,6},{6,7},{7,8},{8,9},{9,10},{10,1... | collective-permute-start | bytes 24584 | tf_op jit(solution)/shard_map/ppermute | solution.py:18
  97.9 3.8 %copy-start.4 = (f32[4,384,1]{2,1,0:T(8,128)S(1)}, f32[4,384,1]{2,1,0:T(8,128)}, u32[]{:S(2)}) copy-start(f32[4,384,1]{2,1,0:T(8,128)} %copy.12) | copy-start | bytes 18436
  97.9 3.8 %copy-start.5 = (f32[4,384,1]{2,1,0:T(8,128)S(1)}, f32[4,384,1]{2,1,0:T(8,128)}, u32[]{:S(2)}) copy-start(f32[4,384,1]{2,1,0:T(8,128)} %copy.14) | copy-start | bytes 18436
  104.4 2.6 %copy-start.6 = (bf16[384,512]{1,0:T(8,128)(2,1)S(1)}, bf16[384,512]{1,0:T(8,128)(2,1)}, u32[]{:S(2)}) copy-start(bf16[384,512]{1,0:T(8,128)(2,1)} %param.13) | copy-start | bytes 1179652
where the time goes:
time: 111 us
  waiting for transfers between devices  40.7 us (37%)
  starting transfers between devices  33.9 us (31%)
  matrix products  14.9 us (13%)
  other arithmetic  14.4 us (13%)
  local copies, waits for them, and re-layouts  6.25 us (6%)
    ppermute x4, waiting for transfers between devices, passed_along(): return lax.ppermute(value, axis, pairs)  34 us
    ppermute x3, starting transfers between devices, padded(): lax.ppermute(lax.slice_in_dim(block, block.shape[dim] - width, None, axis...  17.6 us
    dot_general x5, matrix products, green_term(): jnp.dot(radial, green_azimuth[offset + 2], preferred_element_type=jnp.flo...  14.9 us
    ppermute x4, starting transfers between devices, passed_along(): return lax.ppermute(value, axis, pairs)  10.7 us
    ppermute x3, starting transfers between devices, padded(): lax.ppermute(lax.slice_in_dim(block, 0, width, axis=dim), axis, backward)  5.66 us
    concatenate x2, other arithmetic, padded(): block = jnp.concatenate([low, block, high], axis=dim)  4.92 us
    ppermute x3, waiting for transfers between devices, padded(): lax.ppermute(lax.slice_in_dim(block, 0, width, axis=dim), axis, backward)  3.64 us
    ppermute x3, waiting for transfers between devices, padded(): lax.ppermute(lax.slice_in_dim(block, block.shape[dim] - width, None, axis...  3.06 us
  transfers between devices with their start and end apart: 10, of which 4 were waited for; matrix products, arithmetic and copies ran while one was open for 19% of the time, Pallas kernels for 0%

commit v1 on v0

v1 whole, which is shorter than its diff:
```python
import functools

import jax
import jax.numpy as jnp
from jax import lax
from jax.experimental import pallas as pl
from jax.experimental.pallas import tpu as pltpu
from jax.sharding import PartitionSpec as P

diffusion = 0.1
gravity = 0.1
kepler = 0.6

MESH = pl.DeviceIdType.MESH
F32 = jnp.float32
BF16 = jnp.bfloat16


def kernel(
    chunk,
    strip,
    gas,
    green_radial,
    green_azimuth,
    dust_density,
    dust_radial,
    dust_azimuth,
    coupling,
    potential,
    density_next,
    radial_next,
    azimuth_next,
    ext,
    gr,
    ga,
    fld,
    kv,
    potp,
    near,
    far_out,
    far_in,
    part_out,
    part_in,
    dcol_out,
    dcol_in,
    dcol,
    pcol_out,
    pcol_in,
    pcol,
    load_sem,
    gas_send,
    gas_recv,
    drow_send,
    drow_recv,
    dcol_send,
    dcol_recv,
    far_send,
    far_recv,
    part_send,
    part_recv,
    prow_send,
    prow_recv,
    pcol_send,
    pcol_recv,
):
    rows, arc = dust_density.shape
    chunks = rows // chunk
    band = lax.axis_index("band")
    sector = lax.axis_index("sector")
    bands = lax.axis_size("band")
    sectors = lax.axis_size("sector")
    ahead = lax.rem(sector + 1, sectors)
    behind = lax.rem(sector + sectors - 1, sectors)
    has_up = band < bands - 1
    has_down = band > 0
    side = (ahead, behind)

    def load(src, dst, n):
        copy = pltpu.make_async_copy(src, dst, load_sem.at[n])
        copy.start()
        return copy

    own = pl.ds(rows, rows)
    body_rows = pl.ds(8, rows)
    load_fields = [
        load(field, fld.at[n, body_rows, :], n)
        for n, field in enumerate((dust_density, dust_radial, dust_azimuth))
    ]
    load_gas = load(gas, ext.at[own, :], 3)
    load_gr = {}
    for n, j in enumerate((4, 0, 2, 3, 1)):
        load_gr[j] = load(green_radial.at[j], gr.at[j], 4 + n)
    load_ga = load(green_azimuth, ga, 9)
    load_k = load(coupling, kv, 10)

    barrier = pltpu.get_barrier_semaphore()
    for s in side:
        pl.semaphore_signal(barrier, inc=1, device_id={"sector": s}, device_id_type=MESH)

    @pl.when(has_up)
    def _():
        pl.semaphore_signal(barrier, inc=1, device_id={"band": band + 1}, device_id_type=MESH)

    @pl.when(has_down)
    def _():
        pl.semaphore_signal(barrier, inc=1, device_id={"band": band - 1}, device_id_type=MESH)

    pl.semaphore_wait(
        barrier, 2 + has_up.astype(jnp.int32) + has_down.astype(jnp.int32)
    )

    def remote(src, dst, send, recv, where):
        return pltpu.make_async_remote_copy(
            src_ref=src,
            dst_ref=dst,
            send_sem=send,
            recv_sem=recv,
            device_id=where,
            device_id_type=MESH,
        )

    up = {"band": band + 1}
    down = {"band": band - 1}
    gas_up = remote(gas, ext.at[pl.ds(0, rows), :], gas_send.at[0], gas_recv.at[0], up)
    gas_down = remote(gas, ext.at[pl.ds(2 * rows, rows), :], gas_send.at[1], gas_recv.at[1], down)
    top = pl.ds(rows, 8)
    bottom = pl.ds(8, 8)
    halo_low = pl.ds(0, 8)
    halo_high = pl.ds(rows + 8, 8)
    drow_up = remote(
        fld.at[:, top, :], fld.at[:, halo_low, :], drow_send.at[0], drow_recv.at[0], up
    )
    drow_down = remote(
        fld.at[:, bottom, :], fld.at[:, halo_high, :], drow_send.at[1], drow_recv.at[1], down
    )
    prow_up = remote(
        potp.at[top, :], potp.at[halo_low, :], prow_send.at[0], prow_recv.at[0], up
    )
    prow_down = remote(
        potp.at[bottom, :], potp.at[halo_high, :], prow_send.at[1], prow_recv.at[1], down
    )

    @pl.when(has_up)
    def _():
        gas_up.start()

    @pl.when(has_down)
    def _():
        gas_down.start()

    @pl.when(jnp.logical_not(has_down))
    def _():
        ext[0:rows, :] = jnp.zeros((rows, arc), BF16)
        fld[:, 0:8, :] = jnp.zeros((3, 8, arc), F32)
        potp[0:8, :] = jnp.zeros((8, arc), F32)

    @pl.when(jnp.logical_not(has_up))
    def _():
        ext[2 * rows : 3 * rows, :] = jnp.zeros((rows, arc), BF16)
        fld[:, rows + 8 : rows + 16, :] = jnp.zeros((3, 8, arc), F32)
        potp[rows + 8 : rows + 16, :] = jnp.zeros((8, arc), F32)

    for copy in load_fields:
        copy.wait()

    @pl.when(has_up)
    def _():
        drow_up.start()

    @pl.when(has_down)
    def _():
        drow_down.start()

    for d, first in ((0, arc - 128), (1, 0)):
        lane = 127 if d == 0 else 0
        for n in range(3):
            turned = jnp.transpose(fld[n, 8 : 8 + rows, first : first + 128])
            dcol_out[d, n : n + 1, :] = turned[lane : lane + 1, :]
        dcol_out[d, 3:8, :] = jnp.zeros((5, rows), F32)
    dcol_copies = [
        remote(
            dcol_out.at[d], dcol_in.at[d], dcol_send.at[d], dcol_recv.at[d], {"sector": side[d]}
        )
        for d in range(2)
    ]
    for copy in dcol_copies:
        copy.start()

    def far_copy(d, c):
        part = pl.ds(pl.multiple_of(c * chunk, chunk), chunk)
        return remote(
            far_out.at[d, part, :],
            far_in.at[d, part, :],
            far_send.at[d, c],
            far_recv.at[d, c],
            {"sector": side[d]},
        )

    def part_copy(d, c):
        part = pl.ds(pl.multiple_of(c * chunk, chunk), chunk)
        return remote(
            part_out.at[d, part, :],
            part_in.at[d, part, :],
            part_send.at[d, c],
            part_recv.at[d, c],
            {"sector": side[d]},
        )

    def pcol_copy(d, c):
        return remote(
            pcol_out.at[d, c],
            pcol_in.at[d, c],
            pcol_send.at[d, c],
            pcol_recv.at[d, c],
            {"sector": side[d]},
        )

    def nth(step):
        return lax.rem(chunks - step, chunks)

    load_gas.wait()
    load_gr[4].wait()
    load_gr[0].wait()

    @pl.when(has_up)
    def _():
        gas_up.wait_send()
        gas_down.wait_recv()

    @pl.when(has_down)
    def _():
        gas_down.wait_send()
        gas_up.wait_recv()

    @pl.loop(0, chunks)
    def _(step):
        c = nth(step)
        part = pl.ds(pl.multiple_of(c * chunk, chunk), chunk)
        for d, j in ((0, 4), (1, 0)):
            far_out[d, part, :] = jnp.dot(
                gr[j, part, :], ext[...], preferred_element_type=F32
            ).astype(BF16)
            far_copy(d, c).start()

    for j in (2, 3, 1):
        load_gr[j].wait()
    load_ga.wait()

    @pl.loop(0, chunks)
    def _(step):
        c = nth(step)
        part = pl.ds(pl.multiple_of(c * chunk, chunk), chunk)
        for d, j in ((0, 3), (1, 1)):
            near[d, part, :] = jnp.dot(
                gr[j, part, :], ext[...], preferred_element_type=F32
            ).astype(BF16)

    @pl.loop(0, chunks)
    def _(step):
        c = nth(step)
        part = pl.ds(pl.multiple_of(c * chunk, chunk), chunk)
        for d, j in ((0, 3), (1, 1)):
            close = jnp.dot(near[d, part, :], ga[j], preferred_element_type=F32)
            far_copy(d, c).wait_recv()
            total = close + jnp.dot(
                far_in[d, part, :], ga[4 - 4 * d], preferred_element_type=F32
            )
            part_out[d, part, :] = total.astype(BF16)
            part_copy(d, c).start()

    @pl.loop(0, chunks)
    def _(step):
        c = nth(step)
        part = pl.ds(pl.multiple_of(c * chunk, chunk), chunk)
        mid = jnp.dot(gr[2, part, :], ext[...], preferred_element_type=F32).astype(BF16)
        potential[part, :] = jnp.dot(mid, ga[2], preferred_element_type=F32)

    load_k.wait()
    for copy in dcol_copies:
        copy.wait()

    @pl.when(has_up)
    def _():
        drow_up.wait_send()
        drow_down.wait_recv()

    @pl.when(has_down)
    def _():
        drow_down.wait_send()
        drow_up.wait_recv()

    for d in range(2):
        dcol[d] = jnp.transpose(
            jnp.concatenate([dcol_in[d], jnp.zeros((120, rows), F32)], axis=0)
        )

    total_rows = rows * bands

    def inverse_radius(first, count):
        index = first + lax.broadcasted_iota(jnp.int32, (count, 1), 0)
        return 1.0 / (1.0 + 3.0 * (index.astype(F32) + 0.5) / total_rows)

    lanes = lax.broadcasted_iota(jnp.int32, (strip, arc), 1)
    is_first = lanes == 0
    is_last = lanes == arc - 1

    @pl.loop(0, rows // strip)
    def _(step):
        first = pl.multiple_of(step * strip, strip)
        part = pl.ds(first, strip)
        window = pl.ds(first, strip + 16)
        inv = inverse_radius(band * rows + first, strip)
        west_edge = dcol[0, part, :]
        east_edge = dcol[1, part, :]
        centre, above, below, east, west = [], [], [], [], []
        for n in range(3):
            q = fld[n, window, :]
            mid = q[8 : 8 + strip]
            centre.append(mid)
            above.append(q[9 : 9 + strip])
            below.append(q[7 : 7 + strip])
            east.append(jnp.where(is_last, east_edge[:, n : n + 1], pltpu.roll(mid, arc - 1, 1)))
            west.append(jnp.where(is_first, west_edge[:, n : n + 1], pltpu.roll(mid, 1, 1)))
        rho, u, w = centre
        k = kv[part, :].astype(F32)
        lap = [above[n] + below[n] + east[n] + west[n] - 4.0 * centre[n] for n in range(3)]
        density_next[part, :] = (
            rho
            - 0.5 * (above[0] * above[1] - below[0] * below[1])
            - 0.5 * inv * (east[0] * east[2] - west[0] * west[2])
            + diffusion * lap[0]
        )
        radial_next[part, :] = (
            u
            - 0.5 * u * (above[1] - below[1])
            - 0.5 * inv * w * (east[1] - west[1])
            - k * u
            + diffusion * lap[1]
        )
        azimuth_next[part, :] = (
            w
            - 0.5 * u * (above[2] - below[2])
            - 0.5 * inv * w * (east[2] - west[2])
            - k * (w - kepler * jnp.sqrt(inv))
            + diffusion * lap[2]
        )

    @pl.loop(0, chunks)
    def _(step):
        c = nth(step)
        part = pl.ds(pl.multiple_of(c * chunk, chunk), chunk)
        for d in range(2):
            part_copy(d, c).wait_recv()
        total = potential[part, :] + (part_in[0, part, :].astype(F32) + part_in[1, part, :].astype(F32))
        potential[part, :] = total
        potp[pl.ds(pl.multiple_of(c * chunk + 8, 8), chunk), :] = total
        for d, first in ((0, arc - 128), (1, 0)):
            lane = 127 if d == 0 else 0
            turned = jnp.transpose(total[:, first : first + 128])
            pcol_out[d, c, 0:1, :] = turned[lane : lane + 1, :]
            pcol_copy(d, c).start()

        @pl.when(jnp.logical_and(c == chunks - 1, has_up))
        def _():
            prow_up.start()

        @pl.when(jnp.logical_and(c == 0, has_down))
        def _():
            prow_down.start()

    @pl.when(has_up)
    def _():
        prow_up.wait_send()
        prow_down.wait_recv()

    @pl.when(has_down)
    def _():
        prow_down.wait_send()
        prow_up.wait_recv()

    lanes_c = lax.broadcasted_iota(jnp.int32, (chunk, arc), 1)
    first_c = lanes_c == 0
    last_c = lanes_c == arc - 1

    @pl.loop(0, chunks)
    def _(step):
        c = nth(step)
        first = pl.multiple_of(c * chunk, chunk)
        part = pl.ds(first, chunk)
        window = pl.ds(first, chunk + 16)
        inv = inverse_radius(band * rows + first, chunk)
        q = potp[window, :]
        mid = q[8 : 8 + chunk]
        for d in range(2):
            pcol_copy(d, c).wait()
            far_copy(d, c).wait_send()
            part_copy(d, c).wait_send()
        edges = []
        for d in range(2):
            full = jnp.concatenate([pcol_in[d, c], jnp.zeros((120, chunk), F32)], axis=0)
            edges.append(jnp.transpose(full)[:, 0:1])
        east = jnp.where(last_c, edges[1], pltpu.roll(mid, arc - 1, 1))
        west = jnp.where(first_c, edges[0], pltpu.roll(mid, 1, 1))
        radial_next[part, :] = radial_next[part, :] - 0.5 * gravity * (
            q[9 : 9 + chunk] - q[7 : 7 + chunk]
        )
        azimuth_next[part, :] = azimuth_next[part, :] - 0.5 * gravity * inv * (east - west)


def body(gas, green_radial, green_azimuth, rho, u, w, coupling, chunk, strip):
    rows, arc = rho.shape
    chunks = rows // chunk
    dma = pltpu.SemaphoreType.DMA
    out = [pltpu.VMEM((rows, arc), F32)] * 4
    return pl.pallas_call(
        functools.partial(kernel, chunk, strip),
        out_shape=out,
        in_specs=[pl.BlockSpec(memory_space=pl.ANY)] * 7,
        out_specs=[pl.BlockSpec(memory_space=pltpu.VMEM)] * 4,
        scratch_shapes=[
            pltpu.VMEM((3 * rows, arc), BF16),
            pltpu.VMEM((5, rows, 3 * rows), BF16),
            pltpu.VMEM((5, arc, arc), BF16),
            pltpu.VMEM((3, rows + 16, arc), F32),
            pltpu.VMEM((rows, arc), BF16),
            pltpu.VMEM((rows + 16, arc), F32),
            pltpu.VMEM((2, rows, arc), BF16),
            pltpu.VMEM((2, rows, arc), BF16),
            pltpu.VMEM((2, rows, arc), BF16),
            pltpu.VMEM((2, rows, arc), BF16),
            pltpu.VMEM((2, rows, arc), BF16),
            pltpu.VMEM((2, 8, rows), F32),
            pltpu.VMEM((2, 8, rows), F32),
            pltpu.VMEM((2, rows, 128), F32),
            pltpu.VMEM((2, chunks, 8, chunk), F32),
            pltpu.VMEM((2, chunks, 8, chunk), F32),
            pltpu.VMEM((2, rows, 128), F32),
            dma((11,)),
            dma((2,)),
            dma((2,)),
            dma((2,)),
            dma((2,)),
            dma((2,)),
            dma((2,)),
            dma((2, chunks)),
            dma((2, chunks)),
            dma((2, chunks)),
            dma((2, chunks)),
            dma((2,)),
            dma((2,)),
            dma((2, chunks)),
            dma((2, chunks)),
        ],
        compiler_params=pltpu.CompilerParams(
            collective_id=0, has_side_effects=True, vmem_limit_bytes=56 * 2**20
        ),
        name="disc",
    )(gas, green_radial, green_azimuth, rho, u, w, coupling)


def solution(mesh, chunk=128, strip=32):
    return jax.shard_map(
        functools.partial(body, chunk=chunk, strip=strip),
        mesh=mesh,
        in_specs=(
            P("band", "sector"),
            P(None, "band", None),
            P(),
            P("band", "sector"),
            P("band", "sector"),
            P("band", "sector"),
            P("band", "sector"),
        ),
        out_specs=(P("band", "sector"),) * 4,
        check_vma=False,
    )
```

time: 111 us -> 46.5 us (0.42)
  the two profiles are of different devices: /device:TPU:1 before, /device:TPU:7 now
where the time goes in v1:
time: 46.5 us; the launch traced here: 46.4 us
  Pallas kernels  42.3 us (91%)
  local copies, waits for them, and re-layouts  3.52 us (8%)
  between operations  0.64 us (1%)
    pallas_call x1, Pallas kernels, body(): pl.pallas_call(functools.partial(kernel, chunk, strip), out_shape=out, in...  42.3 us
    unnamed x4, local copies, waits for them, and re-layouts  3.52 us

profile of v1, /device:TPU:7, one launch (start us, length us, event | category | flops | bytes accessed | tf_op | source)
XLA Modules:
  0.0 46.4 jit_solution(13576806333968607861)
XLA Ops:
  0.6 42.3 %disc.1 = (f32[384,512]{1,0:T(8,128)S(1)}, f32[384,512]{1,0:T(8,128)S(1)}, f32[384,512]{1,0:T(8,128)S(1)}, f32[384,512]{1,0:T(8,128)S(1)}) custom-call(bf16[384,512]{1,0:T(8,128)(2,1)} %gas.1, bf16[5,384,1152]{2,1,0:T(8,128)(2,1)} %green_radial.1, bf16[5,512,512]{2,1,0:T(8,128)(2,1)} %green_azimuth.1, f32[384,512]{1,0:T(8,128)} %dust_density.1, ...), custom_call_target="tpu_custom_call" | custom-call | tf_op jit(solution)/shard_map/disc/pallas_call | solution.py:415
  42.9 0.9 %copy.15 = f32[384,512]{1,0:T(8,128)} copy(f32[384,512]{1,0:T(8,128)S(1)} %get-tuple-element.4) | data formatting | bytes 1572864
  43.8 0.9 %copy.16 = f32[384,512]{1,0:T(8,128)} copy(f32[384,512]{1,0:T(8,128)S(1)} %get-tuple-element.5) | data formatting | bytes 1572864
  44.7 0.9 %copy.17 = f32[384,512]{1,0:T(8,128)} copy(f32[384,512]{1,0:T(8,128)S(1)} %get-tuple-element.6) | data formatting | bytes 1572864
  45.5 0.9 %copy.18 = f32[384,512]{1,0:T(8,128)} copy(f32[384,512]{1,0:T(8,128)S(1)} %get-tuple-element.7) | data formatting | bytes 1572864

commit v2 on v1

v2 whole, which is shorter than its diff:
```python
import functools

import jax
import jax.numpy as jnp
from jax import lax
from jax.experimental import pallas as pl
from jax.experimental.pallas import tpu as pltpu
from jax.sharding import PartitionSpec as P

diffusion = 0.1
gravity = 0.1
kepler = 0.6

MESH = pl.DeviceIdType.MESH
F32 = jnp.float32
BF16 = jnp.bfloat16


def kernel(
    chunk,
    strip,
    pieces,
    gas,
    green_radial,
    green_azimuth,
    dust_density,
    dust_radial,
    dust_azimuth,
    coupling,
    potential,
    density_next,
    radial_next,
    azimuth_next,
    ext,
    gr,
    ga,
    fld,
    kv,
    potp,
    near,
    far_out,
    far_in,
    part_out,
    part_in,
    col_out,
    col_in,
    col_own,
    dcol,
    load_sem,
    gas_send,
    gas_recv,
    row_send,
    row_recv,
    col_send,
    col_recv,
    far_send,
    far_recv,
    part_send,
    part_recv,
):
    rows, arc = dust_density.shape
    chunks = rows // chunk
    band = lax.axis_index("band")
    sector = lax.axis_index("sector")
    bands = lax.axis_size("band")
    sectors = lax.axis_size("sector")
    side = (lax.rem(sector + 1, sectors), lax.rem(sector + sectors - 1, sectors))
    side_two = (lax.rem(sector + 2, sectors), lax.rem(sector + sectors - 2, sectors))
    has_up = band < bands - 1
    has_down = band > 0

    def load(src, dst, n):
        copy = pltpu.make_async_copy(src, dst, load_sem.at[n])
        copy.start()
        return copy

    own = pl.ds(rows, rows)
    body_rows = pl.ds(8, rows)
    load_gas = load(gas, ext.at[own, :], 3)
    load_gr = {}
    for n, j in enumerate((4, 0)):
        load_gr[j] = load(green_radial.at[j], gr.at[j], 4 + n)
    load_fields = [
        load(field, fld.at[n, body_rows, :], n)
        for n, field in enumerate((dust_density, dust_radial, dust_azimuth))
    ]
    for n, j in enumerate((3, 1)):
        load_gr[j] = load(green_radial.at[j], gr.at[j], 6 + n)
    load_ga = load(green_azimuth, ga, 9)
    load_gr[2] = load(green_radial.at[2], gr.at[2], 8)
    load_k = load(coupling, kv, 10)

    barrier = pltpu.get_barrier_semaphore()
    for s in side + side_two:
        pl.semaphore_signal(barrier, inc=1, device_id={"sector": s}, device_id_type=MESH)

    @pl.when(has_up)
    def _():
        pl.semaphore_signal(barrier, inc=1, device_id={"band": band + 1}, device_id_type=MESH)

    @pl.when(has_down)
    def _():
        pl.semaphore_signal(barrier, inc=1, device_id={"band": band - 1}, device_id_type=MESH)

    pl.semaphore_wait(barrier, 4 + has_up.astype(jnp.int32) + has_down.astype(jnp.int32))

    def remote(src, dst, send, recv, where):
        return pltpu.make_async_remote_copy(
            src_ref=src,
            dst_ref=dst,
            send_sem=send,
            recv_sem=recv,
            device_id=where,
            device_id_type=MESH,
        )

    up = {"band": band + 1}
    down = {"band": band - 1}

    def gas_copies(n):
        cols = pl.ds(*pieces[n])
        return (
            remote(
                gas.at[:, cols],
                ext.at[pl.ds(0, rows), cols],
                gas_send.at[0, n],
                gas_recv.at[0, n],
                up,
            ),
            remote(
                gas.at[:, cols],
                ext.at[pl.ds(2 * rows, rows), cols],
                gas_send.at[1, n],
                gas_recv.at[1, n],
                down,
            ),
        )

    def start_both(copies):
        @pl.when(has_up)
        def _():
            copies[0].start()

        @pl.when(has_down)
        def _():
            copies[1].start()

    def wait_both(copies):
        @pl.when(has_up)
        def _():
            copies[0].wait_send()
            copies[1].wait_recv()

        @pl.when(has_down)
        def _():
            copies[1].wait_send()
            copies[0].wait_recv()

    for n in range(len(pieces)):
        start_both(gas_copies(n))

    top = pl.ds(rows, 8)
    bottom = pl.ds(8, 8)
    halo_low = pl.ds(0, 8)
    halo_high = pl.ds(rows + 8, 8)
    drow = (
        remote(fld.at[:, top, :], fld.at[:, halo_low, :], row_send.at[0], row_recv.at[0], up),
        remote(fld.at[:, bottom, :], fld.at[:, halo_high, :], row_send.at[1], row_recv.at[1], down),
    )
    prow = (
        remote(potp.at[top, :], potp.at[halo_low, :], row_send.at[2], row_recv.at[2], up),
        remote(potp.at[bottom, :], potp.at[halo_high, :], row_send.at[3], row_recv.at[3], down),
    )

    @pl.when(jnp.logical_not(has_down))
    def _():
        ext[0:rows, :] = jnp.zeros((rows, arc), BF16)
        fld[:, 0:8, :] = jnp.zeros((3, 8, arc), F32)
        potp[0:8, :] = jnp.zeros((8, arc), F32)

    @pl.when(jnp.logical_not(has_up))
    def _():
        ext[2 * rows : 3 * rows, :] = jnp.zeros((rows, arc), BF16)
        fld[:, rows + 8 : rows + 16, :] = jnp.zeros((3, 8, arc), F32)
        potp[rows + 8 : rows + 16, :] = jnp.zeros((8, arc), F32)

    def col_copy(kind, d):
        where = side_two[d] if kind == 2 else side[d]
        return remote(
            col_out.at[kind, d],
            col_in.at[kind, d],
            col_send.at[kind, d],
            col_recv.at[kind, d],
            {"sector": where},
        )

    def edge(tile, d):
        lane = 127 if d == 0 else 0
        return jnp.transpose(tile)[lane : lane + 1, :]

    def edge_tile(d):
        return slice(arc - 128, arc) if d == 0 else slice(0, 128)

    for copy in load_fields:
        copy.wait()
    start_both(drow)
    for d in range(2):
        for n in range(3):
            col_out[0, d, n : n + 1, :] = edge(fld[n, 8 : 8 + rows, edge_tile(d)], d)
        col_copy(0, d).start()

    def far_copy(d, n):
        if n < len(pieces) - 1:
            part, cols = pl.ds(0, rows), pl.ds(*pieces[n])
        else:
            c = n - (len(pieces) - 1)
            part, cols = pl.ds(c * chunk, chunk), pl.ds(*pieces[-1])
        return remote(
            far_out.at[d, part, cols],
            far_in.at[d, part, cols],
            far_send.at[d, n],
            far_recv.at[d, n],
            {"sector": side[d]},
        )

    def part_copy(d, c):
        part = pl.ds(c * chunk, chunk)
        return remote(
            part_out.at[d, part, :],
            part_in.at[d, part, :],
            part_send.at[d, c],
            part_recv.at[d, c],
            {"sector": side[d]},
        )

    order = [(chunks - n) % chunks for n in range(chunks)]
    whole = len(pieces) - 1
    load_gas.wait()
    load_gr[4].wait()
    load_gr[0].wait()
    for n in range(whole):
        wait_both(gas_copies(n))
        cols = slice(pieces[n][0], pieces[n][0] + pieces[n][1])
        for d, j in ((0, 4), (1, 0)):
            far_out[d, :, cols] = jnp.dot(
                gr[j], ext[:, cols], preferred_element_type=F32
            ).astype(BF16)
            far_copy(d, n).start()
    wait_both(gas_copies(whole))
    last = slice(pieces[-1][0], arc)
    for c in order:
        part = slice(c * chunk, (c + 1) * chunk)
        for d, j in ((0, 4), (1, 0)):
            far_out[d, part, last] = jnp.dot(
                gr[j, part, :], ext[:, last], preferred_element_type=F32
            ).astype(BF16)
            far_copy(d, whole + c).start()

    load_gr[3].wait()
    load_gr[1].wait()
    load_ga.wait()
    for d, j in ((0, 3), (1, 1)):
        near[d] = jnp.dot(gr[j], ext[...], preferred_element_type=F32).astype(BF16)

    load_k.wait()
    for d in range(2):
        col_copy(0, d).wait()
    wait_both(drow)

    def columns(block):
        return jnp.transpose(jnp.concatenate([block, jnp.zeros((120, rows), F32)], axis=0))

    for d in range(2):
        dcol[d] = columns(col_in[0, d])

    total_rows = rows * bands

    def inverse_radius(first, count):
        index = first + lax.broadcasted_iota(jnp.int32, (count, 1), 0)
        return 1.0 / (1.0 + 3.0 * (index.astype(F32) + 0.5) / total_rows)

    def dust(start, stop):
        lanes = lax.broadcasted_iota(jnp.int32, (strip, arc), 1)
        is_first = lanes == 0
        is_last = lanes == arc - 1

        @pl.loop(start // strip, stop // strip)
        def _(step):
            first = pl.multiple_of(step * strip, strip)
            part = pl.ds(first, strip)
            window = pl.ds(first, strip + 16)
            inv = inverse_radius(band * rows + first, strip)
            west_edge = dcol[0, part, :]
            east_edge = dcol[1, part, :]
            centre, above, below, east, west = [], [], [], [], []
            for n in range(3):
                q = fld[n, window, :]
                mid = q[8 : 8 + strip]
                centre.append(mid)
                above.append(q[9 : 9 + strip])
                below.append(q[7 : 7 + strip])
                east.append(
                    jnp.where(is_last, east_edge[:, n : n + 1], pltpu.roll(mid, arc - 1, 1))
                )
                west.append(jnp.where(is_first, west_edge[:, n : n + 1], pltpu.roll(mid, 1, 1)))
            rho, u, w = centre
            k = kv[part, :].astype(F32)
            lap = [above[n] + below[n] + east[n] + west[n] - 4.0 * centre[n] for n in range(3)]
            density_next[part, :] = (
                rho
                - 0.5 * (above[0] * above[1] - below[0] * below[1])
                - 0.5 * inv * (east[0] * east[2] - west[0] * west[2])
                + diffusion * lap[0]
            )
            radial_next[part, :] = (
                u
                - 0.5 * u * (above[1] - below[1])
                - 0.5 * inv * w * (east[1] - west[1])
                - k * u
                + diffusion * lap[1]
            )
            azimuth_next[part, :] = (
                w
                - 0.5 * u * (above[2] - below[2])
                - 0.5 * inv * w * (east[2] - west[2])
                - k * (w - kepler * jnp.sqrt(inv))
                + diffusion * lap[2]
            )

    dust(0, rows // 2)

    for d in range(2):
        for n in range(whole):
            far_copy(d, n).wait_recv()
    for c in order:
        part = slice(c * chunk, (c + 1) * chunk)
        for d, j in ((0, 3), (1, 1)):
            far_copy(d, whole + c).wait_recv()
            total = jnp.dot(near[d, part, :], ga[j], preferred_element_type=F32) + jnp.dot(
                far_in[d, part, :], ga[4 - 4 * d], preferred_element_type=F32
            )
            part_out[d, part, :] = total.astype(BF16)
            part_copy(d, c).start()

    for d in range(2):
        col_out[2, d, 0:1, :] = edge(part_out[d, :, edge_tile(d)].astype(F32), d)
        col_copy(2, d).start()
        col_own[1 - d, 0:1, :] = edge(part_out[d, :, edge_tile(1 - d)].astype(F32), 1 - d)

    load_gr[2].wait()
    middle = jnp.dot(gr[2], ext[...], preferred_element_type=F32).astype(BF16)
    potential[...] = jnp.dot(middle, ga[2], preferred_element_type=F32)
    for d in range(2):
        col_out[1, d, 0:1, :] = edge(potential[:, edge_tile(d)], d)
        col_copy(1, d).start()

    dust(rows // 2, rows)

    for d in range(2):
        col_copy(1, d).wait()
        col_copy(2, d).wait()
        row = col_in[1, d, 0:1, :] + (col_in[2, d, 0:1, :] + col_own[d, 0:1, :])
        dcol[d] = jnp.transpose(jnp.concatenate([row, jnp.zeros((127, rows), F32)], axis=0))

    lanes = lax.broadcasted_iota(jnp.int32, (chunk, arc), 1)
    is_first = lanes == 0
    is_last = lanes == arc - 1
    for c in order:
        part = slice(c * chunk, (c + 1) * chunk)
        for d in range(2):
            part_copy(d, c).wait_recv()
        total = potential[part, :] + (
            part_in[0, part, :].astype(F32) + part_in[1, part, :].astype(F32)
        )
        potential[part, :] = total
        potp[8 + c * chunk : 8 + (c + 1) * chunk, :] = total
        if c == 0:

            @pl.when(has_down)
            def _():
                prow[1].start()

        if c == chunks - 1:

            @pl.when(has_up)
            def _():
                prow[0].start()

        inv = inverse_radius(band * rows + c * chunk, chunk)
        east = jnp.where(is_last, dcol[1, part, 0:1], pltpu.roll(total, arc - 1, 1))
        west = jnp.where(is_first, dcol[0, part, 0:1], pltpu.roll(total, 1, 1))
        azimuth_next[part, :] = azimuth_next[part, :] - 0.5 * gravity * inv * (east - west)

    wait_both(prow)
    for c in order:
        part = slice(c * chunk, (c + 1) * chunk)
        q = potp[c * chunk : (c + 1) * chunk + 16, :]
        radial_next[part, :] = radial_next[part, :] - 0.5 * gravity * (
            q[9 : 9 + chunk] - q[7 : 7 + chunk]
        )
    for d in range(2):
        for n in range(whole + chunks):
            far_copy(d, n).wait_send()
        for c in range(chunks):
            part_copy(d, c).wait_send()


def hand_over(*refs):
    copies = [
        pltpu.make_async_copy(refs[n], refs[4 + n], refs[8].at[n]) for n in range(4)
    ]
    for copy in copies:
        copy.start()
    for copy in copies:
        copy.wait()


def body(gas, green_radial, green_azimuth, rho, u, w, coupling, chunk, strip, pieces):
    rows, arc = rho.shape
    chunks = rows // chunk
    steps = len(pieces)
    dma = pltpu.SemaphoreType.DMA
    operands = (gas, green_radial, green_azimuth, rho, u, w, coupling)
    results = pl.pallas_call(
        functools.partial(kernel, chunk, strip, pieces),
        out_shape=[pltpu.VMEM((rows, arc), F32)] * 4,
        in_specs=[pl.BlockSpec(memory_space=pltpu.HBM)] * 7,
        out_specs=[pl.BlockSpec(memory_space=pltpu.VMEM)] * 4,
        scratch_shapes=[
            pltpu.VMEM((3 * rows, arc), BF16),
            pltpu.VMEM((5, rows, 3 * rows), BF16),
            pltpu.VMEM((5, arc, arc), BF16),
            pltpu.VMEM((3, rows + 16, arc), F32),
            pltpu.VMEM((rows, arc), BF16),
            pltpu.VMEM((rows + 16, arc), F32),
            pltpu.VMEM((2, rows, arc), BF16),
            pltpu.VMEM((2, rows, arc), BF16),
            pltpu.VMEM((2, rows, arc), BF16),
            pltpu.VMEM((2, rows, arc), BF16),
            pltpu.VMEM((2, rows, arc), BF16),
            pltpu.VMEM((3, 2, 8, rows), F32),
            pltpu.VMEM((3, 2, 8, rows), F32),
            pltpu.VMEM((2, 8, rows), F32),
            pltpu.VMEM((2, rows, 128), F32),
            dma((11,)),
            dma((2, steps)),
            dma((2, steps)),
            dma((4,)),
            dma((4,)),
            dma((3, 2)),
            dma((3, 2)),
            dma((2, steps - 1 + chunks)),
            dma((2, steps - 1 + chunks)),
            dma((2, chunks)),
            dma((2, chunks)),
        ],
        compiler_params=pltpu.CompilerParams(
            collective_id=0, has_side_effects=True, vmem_limit_bytes=50 * 2**20
        ),
        name="disc",
    )(*[pltpu.with_memory_space_constraint(x, pltpu.HBM) for x in operands])
    return pl.pallas_call(
        hand_over,
        out_shape=[jax.ShapeDtypeStruct((rows, arc), F32)] * 4,
        in_specs=[pl.BlockSpec(memory_space=pltpu.VMEM)] * 4,
        out_specs=[pl.BlockSpec(memory_space=pl.ANY)] * 4,
        scratch_shapes=[dma((4,))],
        compiler_params=pltpu.CompilerParams(vmem_limit_bytes=2**20),
        name="hand_over",
    )(*[pltpu.with_memory_space_constraint(r, pltpu.VMEM) for r in results])


def solution(mesh, chunk=96, strip=32, pieces=((0, 128), (128, 128), (256, 256))):
    return jax.shard_map(
        functools.partial(body, chunk=chunk, strip=strip, pieces=pieces),
        mesh=mesh,
        in_specs=(
            P("band", "sector"),
            P(None, "band", None),
            P(),
            P("band", "sector"),
            P("band", "sector"),
            P("band", "sector"),
            P("band", "sector"),
        ),
        out_specs=(P("band", "sector"),) * 4,
        check_vma=False,
    )
```

time: 46.5 us -> 42.3 us (0.910)
  local copies, waits for them, and re-layouts: 3.52 us -> 0 us
  Pallas kernels: 42.3 us -> 41.6 us
    unnamed x4 -> x0, local copies, waits for them, and re-layouts: 3.52 us -> none
    pallas_call x1 -> x2, Pallas kernels: 42.3 us -> 41.6 us  [the longest x1 39.9 us: body(): pl.pallas_call(functools.partial(kernel, chunk, strip, pieces), out_shape...]
where the time goes in v2:
time: 42.3 us
  Pallas kernels  41.6 us (98%)
  between operations  0.64 us (2%)
    pallas_call x1, Pallas kernels, body(): pl.pallas_call(functools.partial(kernel, chunk, strip, pieces), out_shape...  39.9 us
    pallas_call x1, Pallas kernels, body(): pl.pallas_call(hand_over, out_shape=[jax.ShapeDtypeStruct((rows, arc), F3...  1.69 us

profile of v2, /device:TPU:7, one launch (start us, length us, event | category | flops | bytes accessed | tf_op | source)
XLA Modules:
  0.0 42.3 jit_solution(2536881004504315229)
XLA Ops:
  0.6 39.9 %disc.1 = (f32[384,512]{1,0:T(8,128)S(1)}, f32[384,512]{1,0:T(8,128)S(1)}, f32[384,512]{1,0:T(8,128)S(1)}, f32[384,512]{1,0:T(8,128)S(1)}) custom-call(bf16[384,512]{1,0:T(8,128)(2,1)} %gas.1, bf16[5,384,1152]{2,1,0:T(8,128)(2,1)} %green_radial.1, bf16[5,512,512]{2,1,0:T(8,128)(2,1)} %green_azimuth.1, f32[384,512]{1,0:T(8,128)} %dust_density.1, ...), custom_call_target="tpu_custom_call" | custom-call | tf_op jit(solution)/shard_map/disc/pallas_call | solution.py:424
  40.6 1.7 %hand_over.1 = (f32[384,512]{1,0:T(8,128)}, f32[384,512]{1,0:T(8,128)}, f32[384,512]{1,0:T(8,128)}, f32[384,512]{1,0:T(8,128)}) custom-call(f32[384,512]{1,0:T(8,128)S(1)} %get-tuple-element.8.refs_0_, f32[384,512]{1,0:T(8,128)S(1)} %get-tuple-element.9.refs_1_, f32[384,512]{1,0:T(8,128)S(1)} %get-tuple-element.10.refs_2_, ...), custom_call_target="tpu_custom_call" | custom-call | tf_op jit(solution)/shard_map/hand_over/pallas_call | solution.py:462

commit v3 on v2

--- a/solution.py
+++ b/solution.py
@@ -223,8 +223,16 @@
             {"sector": side[d]},
         )
 
+    rim = 16
+
+    def span(c):
+        if c >= chunks:
+            return (0, rim) if c == chunks else (rows - rim, rim)
+        low = c * chunk + (rim if c == 0 else 0)
+        return low, (c + 1) * chunk - (rim if c == chunks - 1 else 0) - low
+
     def part_copy(d, c):
-        part = pl.ds(c * chunk, chunk)
+        part = pl.ds(*span(c))
         return remote(
             part_out.at[d, part, :],
             part_in.at[d, part, :],
@@ -332,10 +340,26 @@
     for d in range(2):
         for n in range(whole):
             far_copy(d, n).wait_recv()
+    def both_rims(block):
+        return jnp.concatenate([block[0:rim, :], block[rows - rim : rows, :]], axis=0)
+
+    for d, j in ((0, 3), (1, 1)):
+        far_copy(d, whole).wait_recv()
+        far_copy(d, whole + chunks - 1).wait_recv()
+        total = (
+            jnp.dot(both_rims(near.at[d]), ga[j], preferred_element_type=F32)
+            + jnp.dot(both_rims(far_in.at[d]), ga[4 - 4 * d], preferred_element_type=F32)
+        ).astype(BF16)
+        part_out[d, 0:rim, :] = total[0:rim]
+        part_out[d, rows - rim : rows, :] = total[rim:]
+        part_copy(d, chunks).start()
+        part_copy(d, chunks + 1).start()
     for c in order:
-        part = slice(c * chunk, (c + 1) * chunk)
+        low, count = span(c)
+        part = slice(low, low + count)
         for d, j in ((0, 3), (1, 1)):
-            far_copy(d, whole + c).wait_recv()
+            if c not in (0, chunks - 1):
+                far_copy(d, whole + c).wait_recv()
             total = jnp.dot(near[d, part, :], ga[j], preferred_element_type=F32) + jnp.dot(
                 far_in[d, part, :], ga[4 - 4 * d], preferred_element_type=F32
             )
@@ -353,6 +377,22 @@
     for d in range(2):
         col_out[1, d, 0:1, :] = edge(potential[:, edge_tile(d)], d)
         col_copy(1, d).start()
+
+    def settle(low, count):
+        part = slice(low, low + count)
+        total = potential[part, :] + (
+            part_in[0, part, :].astype(F32) + part_in[1, part, :].astype(F32)
+        )
+        potential[part, :] = total
+        potp[8 + low : 8 + low + count, :] = total
+        return total
+
+    for d in range(2):
+        part_copy(d, chunks).wait_recv()
+        part_copy(d, chunks + 1).wait_recv()
+    settle(0, rim)
+    settle(rows - rim, rim)
+    start_both(prow)
 
     dust(rows // 2, rows)
 
@@ -369,23 +409,8 @@
         part = slice(c * chunk, (c + 1) * chunk)
         for d in range(2):
             part_copy(d, c).wait_recv()
-        total = potential[part, :] + (
-            part_in[0, part, :].astype(F32) + part_in[1, part, :].astype(F32)
-        )
-        potential[part, :] = total
-        potp[8 + c * chunk : 8 + (c + 1) * chunk, :] = total
-        if c == 0:
-
-            @pl.when(has_down)
-            def _():
-                prow[1].start()
-
-        if c == chunks - 1:
-
-            @pl.when(has_up)
-            def _():
-                prow[0].start()
-
+        settle(*span(c))
+        total = potential[part, :]
         inv = inverse_radius(band * rows + c * chunk, chunk)
         east = jnp.where(is_last, dcol[1, part, 0:1], pltpu.roll(total, arc - 1, 1))
         west = jnp.where(is_first, dcol[0, part, 0:1], pltpu.roll(total, 1, 1))
@@ -401,7 +426,7 @@
     for d in range(2):
         for n in range(whole + chunks):
             far_copy(d, n).wait_send()
-        for c in range(chunks):
+        for c in range(chunks + 2):
             part_copy(d, c).wait_send()
 
 
@@ -451,8 +476,8 @@
             dma((3, 2)),
             dma((2, steps - 1 + chunks)),
             dma((2, steps - 1 + chunks)),
-            dma((2, chunks)),
-            dma((2, chunks)),
+            dma((2, chunks + 2)),
+            dma((2, chunks + 2)),
         ],
         compiler_params=pltpu.CompilerParams(
             collective_id=0, has_side_effects=True, vmem_limit_bytes=50 * 2**20

time: 42.3 us -> 39.3 us (0.929)
  the two profiles are of different devices: /device:TPU:7 before, /device:TPU:1 now
where the time goes in v3:
time: 39.3 us; the launch traced here: 39.2 us
  Pallas kernels  38.6 us (98%)
  between operations  0.64 us (2%)
    pallas_call x1, Pallas kernels, body(): pl.pallas_call(functools.partial(kernel, chunk, strip, pieces), out_shape...  36.9 us
    pallas_call x1, Pallas kernels, body(): pl.pallas_call(hand_over, out_shape=[jax.ShapeDtypeStruct((rows, arc), F3...  1.69 us

profile of v3, /device:TPU:1, one launch (start us, length us, event | category | flops | bytes accessed | tf_op | source)
XLA Modules:
  0.0 39.2 jit_solution(6188223633203486775)
XLA Ops:
  0.6 36.9 %disc.1 = (f32[384,512]{1,0:T(8,128)S(1)}, f32[384,512]{1,0:T(8,128)S(1)}, f32[384,512]{1,0:T(8,128)S(1)}, f32[384,512]{1,0:T(8,128)S(1)}) custom-call(bf16[384,512]{1,0:T(8,128)(2,1)} %gas.1, bf16[5,384,1152]{2,1,0:T(8,128)(2,1)} %green_radial.1, bf16[5,512,512]{2,1,0:T(8,128)(2,1)} %green_azimuth.1, f32[384,512]{1,0:T(8,128)} %dust_density.1, ...), custom_call_target="tpu_custom_call" | custom-call | tf_op jit(solution)/shard_map/disc/pallas_call | solution.py:449
  37.5 1.7 %hand_over.1 = (f32[384,512]{1,0:T(8,128)}, f32[384,512]{1,0:T(8,128)}, f32[384,512]{1,0:T(8,128)}, f32[384,512]{1,0:T(8,128)}) custom-call(f32[384,512]{1,0:T(8,128)S(1)} %get-tuple-element.8.refs_0_, f32[384,512]{1,0:T(8,128)S(1)} %get-tuple-element.9.refs_1_, f32[384,512]{1,0:T(8,128)S(1)} %get-tuple-element.10.refs_2_, ...), custom_call_target="tpu_custom_call" | custom-call | tf_op jit(solution)/shard_map/hand_over/pallas_call | solution.py:487

commit v4 on v3

--- a/solution.py
+++ b/solution.py
@@ -32,6 +32,7 @@
     radial_next,
     azimuth_next,
     ext,
+    gz,
     gr,
     ga,
     fld,
@@ -49,6 +50,8 @@
     load_sem,
     gas_send,
     gas_recv,
+    first_send,
+    first_recv,
     row_send,
     row_recv,
     col_send,
@@ -68,6 +71,11 @@
     side_two = (lax.rem(sector + 2, sectors), lax.rem(sector + sectors - 2, sectors))
     has_up = band < bands - 1
     has_down = band > 0
+    seam_up = band == bands // 2 - 1
+    seam_down = band == bands // 2
+
+    lead = gz.shape[2]
+    whole = len(pieces) - 2
 
     def load(src, dst, n):
         copy = pltpu.make_async_copy(src, dst, load_sem.at[n])
@@ -156,8 +164,53 @@
             copies[1].wait_send()
             copies[0].wait_recv()
 
-    for n in range(len(pieces)):
+    thirds = [pl.ds(n * rows, rows) for n in range(3)]
+
+    def first_copy(d, third, src, where, sent):
+        return remote(
+            src, gz.at[d, thirds[third], :], first_send.at[d, sent], first_recv.at[d, third], where
+        )
+
+    head = pl.ds(0, lead)
+
+    def first_own(d):
+        return first_copy(d, 1, gas.at[:, head], {"sector": side[d]}, 1)
+
+    def first_on(d, third):
+        where = up if third == 0 else down
+        return first_copy(d, third, gz.at[d, thirds[1], :], where, third)
+
+    def first_seam(d, third):
+        return first_copy(d, third, ext.at[thirds[third], head], {"sector": side[d]}, 2 - third)
+
+    for d in range(2):
+        first_own(d).start()
+    def on_seam(up_step, down_step):
+        pl.when(seam_up)(up_step)
+        pl.when(seam_down)(down_step)
+
+    def off_seam(up_step, down_step):
+        pl.when(jnp.logical_and(has_up, jnp.logical_not(seam_up)))(up_step)
+        pl.when(jnp.logical_and(has_down, jnp.logical_not(seam_down)))(down_step)
+
+    def arrive(copies):
+        def from_up():
+            copies[0].wait_send()
+            copies[1].wait_recv()
+
+        def from_down():
+            copies[1].wait_send()
+            copies[0].wait_recv()
+
+        return from_up, from_down
+
+    def leave(copies):
+        return copies[0].start, copies[1].start
+
+    on_seam(*leave(gas_copies(whole + 1)))
+    for n in range(whole + 1):
         start_both(gas_copies(n))
+    off_seam(*leave(gas_copies(whole + 1)))
 
     top = pl.ds(rows, 8)
     bottom = pl.ds(8, 8)
@@ -175,12 +228,14 @@
     @pl.when(jnp.logical_not(has_down))
     def _():
         ext[0:rows, :] = jnp.zeros((rows, arc), BF16)
+        gz[:, 0:rows, :] = jnp.zeros((2, rows, lead), BF16)
         fld[:, 0:8, :] = jnp.zeros((3, 8, arc), F32)
         potp[0:8, :] = jnp.zeros((8, arc), F32)
 
     @pl.when(jnp.logical_not(has_up))
     def _():
         ext[2 * rows : 3 * rows, :] = jnp.zeros((rows, arc), BF16)
+        gz[:, 2 * rows : 3 * rows, :] = jnp.zeros((2, rows, lead), BF16)
         fld[:, rows + 8 : rows + 16, :] = jnp.zeros((3, 8, arc), F32)
         potp[rows + 8 : rows + 16, :] = jnp.zeros((8, arc), F32)
 
@@ -210,11 +265,10 @@
         col_copy(0, d).start()
 
     def far_copy(d, n):
-        if n < len(pieces) - 1:
+        if n < whole:
             part, cols = pl.ds(0, rows), pl.ds(*pieces[n])
         else:
-            c = n - (len(pieces) - 1)
-            part, cols = pl.ds(c * chunk, chunk), pl.ds(*pieces[-1])
+            part, cols = pl.ds((n - whole) * chunk, chunk), pl.ds(*pieces[whole])
         return remote(
             far_out.at[d, part, cols],
             far_in.at[d, part, cols],
@@ -242,10 +296,20 @@
         )
 
     order = [(chunks - n) % chunks for n in range(chunks)]
-    whole = len(pieces) - 1
     load_gas.wait()
     load_gr[4].wait()
     load_gr[0].wait()
+    def pass_on():
+        for d in range(2):
+            first_own(d).wait()
+            off_seam(first_on(d, 0).start, first_on(d, 2).start)
+
+    early = jnp.logical_or(lax.rem(band, 2) == 1, seam_down)
+    pl.when(early)(pass_on)
+    on_seam(*arrive(gas_copies(whole + 1)))
+    for d in range(2):
+        on_seam(first_seam(d, 2).start, first_seam(d, 0).start)
+
     for n in range(whole):
         wait_both(gas_copies(n))
         cols = slice(pieces[n][0], pieces[n][0] + pieces[n][1])
@@ -254,8 +318,9 @@
                 gr[j], ext[:, cols], preferred_element_type=F32
             ).astype(BF16)
             far_copy(d, n).start()
+    pl.when(jnp.logical_not(early))(pass_on)
     wait_both(gas_copies(whole))
-    last = slice(pieces[-1][0], arc)
+    last = slice(pieces[whole][0], pieces[whole][0] + pieces[whole][1])
     for c in order:
         part = slice(c * chunk, (c + 1) * chunk)
         for d, j in ((0, 4), (1, 0)):
@@ -264,11 +329,54 @@
             ).astype(BF16)
             far_copy(d, whole + c).start()
 
+    off_seam(*arrive(gas_copies(whole + 1)))
     load_gr[3].wait()
     load_gr[1].wait()
     load_ga.wait()
     for d, j in ((0, 3), (1, 1)):
         near[d] = jnp.dot(gr[j], ext[...], preferred_element_type=F32).astype(BF16)
+
+    for d, j in ((0, 4), (1, 0)):
+
+        @pl.when(has_up)
+        def _():
+            first_on(d, 0).wait_send()
+            first_on(d, 2).wait_recv()
+
+        @pl.when(has_down)
+        def _():
+            first_on(d, 2).wait_send()
+            first_on(d, 0).wait_recv()
+
+        far_in[d, :, 0:lead] = jnp.dot(gr[j], gz[d], preferred_element_type=F32).astype(BF16)
+    for d in range(2):
+        for n in range(whole):
+            far_copy(d, n).wait_recv()
+    for c in order:
+        part = slice(c * chunk, (c + 1) * chunk)
+        for d, j in ((0, 3), (1, 1)):
+            far_copy(d, whole + c).wait_recv()
+            total = jnp.dot(near[d, part, :], ga[j], preferred_element_type=F32) + jnp.dot(
+                far_in[d, part, :], ga[4 - 4 * d], preferred_element_type=F32
+            )
+            part_out[d, part, :] = total.astype(BF16)
+            if c == 0:
+                part_copy(d, chunks).start()
+            if c == chunks - 1:
+                part_copy(d, chunks + 1).start()
+            part_copy(d, c).start()
+
+    for d in range(2):
+        col_out[2, d, 0:1, :] = edge(part_out[d, :, edge_tile(d)].astype(F32), d)
+        col_copy(2, d).start()
+        col_own[1 - d, 0:1, :] = edge(part_out[d, :, edge_tile(1 - d)].astype(F32), 1 - d)
+
+    load_gr[2].wait()
+    middle = jnp.dot(gr[2], ext[...], preferred_element_type=F32).astype(BF16)
+    potential[...] = jnp.dot(middle, ga[2], preferred_element_type=F32)
+    for d in range(2):
+        col_out[1, d, 0:1, :] = edge(potential[:, edge_tile(d)], d)
+        col_copy(1, d).start()
 
     load_k.wait()
     for d in range(2):
@@ -335,49 +443,6 @@
                 + diffusion * lap[2]
             )
 
-    dust(0, rows // 2)
-
-    for d in range(2):
-        for n in range(whole):
-            far_copy(d, n).wait_recv()
-    def both_rims(block):
-        return jnp.concatenate([block[0:rim, :], block[rows - rim : rows, :]], axis=0)
-
-    for d, j in ((0, 3), (1, 1)):
-        far_copy(d, whole).wait_recv()
-        far_copy(d, whole + chunks - 1).wait_recv()
-        total = (
-            jnp.dot(both_rims(near.at[d]), ga[j], preferred_element_type=F32)
-            + jnp.dot(both_rims(far_in.at[d]), ga[4 - 4 * d], preferred_element_type=F32)
-        ).astype(BF16)
-        part_out[d, 0:rim, :] = total[0:rim]
-        part_out[d, rows - rim : rows, :] = total[rim:]
-        part_copy(d, chunks).start()
-        part_copy(d, chunks + 1).start()
-    for c in order:
-        low, count = span(c)
-        part = slice(low, low + count)
-        for d, j in ((0, 3), (1, 1)):
-            if c not in (0, chunks - 1):
-                far_copy(d, whole + c).wait_recv()
-            total = jnp.dot(near[d, part, :], ga[j], preferred_element_type=F32) + jnp.dot(
-                far_in[d, part, :], ga[4 - 4 * d], preferred_element_type=F32
-            )
-            part_out[d, part, :] = total.astype(BF16)
-            part_copy(d, c).start()
-
-    for d in range(2):
-        col_out[2, d, 0:1, :] = edge(part_out[d, :, edge_tile(d)].astype(F32), d)
-        col_copy(2, d).start()
-        col_own[1 - d, 0:1, :] = edge(part_out[d, :, edge_tile(1 - d)].astype(F32), 1 - d)
-
-    load_gr[2].wait()
-    middle = jnp.dot(gr[2], ext[...], preferred_element_type=F32).astype(BF16)
-    potential[...] = jnp.dot(middle, ga[2], preferred_element_type=F32)
-    for d in range(2):
-        col_out[1, d, 0:1, :] = edge(potential[:, edge_tile(d)], d)
-        col_copy(1, d).start()
-
     def settle(low, count):
         part = slice(low, low + count)
         total = potential[part, :] + (
@@ -394,7 +459,7 @@
     settle(rows - rim, rim)
     start_both(prow)
 
-    dust(rows // 2, rows)
+    dust(0, rows)
 
     for d in range(2):
         col_copy(1, d).wait()
@@ -441,6 +506,7 @@
 
 
 def body(gas, green_radial, green_azimuth, rho, u, w, coupling, chunk, strip, pieces):
+    lead = pieces[-1][1]
     rows, arc = rho.shape
     chunks = rows // chunk
     steps = len(pieces)
@@ -453,6 +519,7 @@
         out_specs=[pl.BlockSpec(memory_space=pltpu.VMEM)] * 4,
         scratch_shapes=[
             pltpu.VMEM((3 * rows, arc), BF16),
+            pltpu.VMEM((2, 3 * rows, lead), BF16),
             pltpu.VMEM((5, rows, 3 * rows), BF16),
             pltpu.VMEM((5, arc, arc), BF16),
             pltpu.VMEM((3, rows + 16, arc), F32),
@@ -470,12 +537,14 @@
             dma((11,)),
             dma((2, steps)),
             dma((2, steps)),
+            dma((2, 3)),
+            dma((2, 3)),
             dma((4,)),
             dma((4,)),
             dma((3, 2)),
             dma((3, 2)),
-            dma((2, steps - 1 + chunks)),
-            dma((2, steps - 1 + chunks)),
+            dma((2, steps - 2 + chunks)),
+            dma((2, steps - 2 + chunks)),
             dma((2, chunks + 2)),
             dma((2, chunks + 2)),
         ],
@@ -495,7 +564,7 @@
     )(*[pltpu.with_memory_space_constraint(r, pltpu.VMEM) for r in results])
 
 
-def solution(mesh, chunk=96, strip=32, pieces=((0, 128), (128, 128), (256, 256))):
+def solution(mesh, chunk=96, strip=32, pieces=((128, 128), (256, 256), (0, 128))):
     return jax.shard_map(
         functools.partial(body, chunk=chunk, strip=strip, pieces=pieces),
         mesh=mesh,

time: 39.3 us -> 38 us (0.967)
  the two profiles are of different devices: /device:TPU:1 before, /device:TPU:7 now
where the time goes in v4:
time: 38 us; the launch traced here: 37.9 us
  Pallas kernels  37.3 us (98%)
  between operations  0.64 us (2%)
    pallas_call x1, Pallas kernels, body(): pl.pallas_call(functools.partial(kernel, chunk, strip, pieces), out_shape...  35.6 us
    pallas_call x1, Pallas kernels, body(): pl.pallas_call(hand_over, out_shape=[jax.ShapeDtypeStruct((rows, arc), F3...  1.69 us

profile of v4, /device:TPU:7, one launch (start us, length us, event | category | flops | bytes accessed | tf_op | source)
XLA Modules:
  0.0 37.9 jit_solution(7893980598452026222)
XLA Ops:
  0.6 35.6 %disc.1 = (f32[384,512]{1,0:T(8,128)S(1)}, f32[384,512]{1,0:T(8,128)S(1)}, f32[384,512]{1,0:T(8,128)S(1)}, f32[384,512]{1,0:T(8,128)S(1)}) custom-call(bf16[384,512]{1,0:T(8,128)(2,1)} %gas.1, bf16[5,384,1152]{2,1,0:T(8,128)(2,1)} %green_radial.1, bf16[5,512,512]{2,1,0:T(8,128)(2,1)} %green_azimuth.1, f32[384,512]{1,0:T(8,128)} %dust_density.1, ...), custom_call_target="tpu_custom_call" | custom-call | tf_op jit(solution)/shard_map/disc/pallas_call | solution.py:515
  36.3 1.7 %hand_over.1 = (f32[384,512]{1,0:T(8,128)}, f32[384,512]{1,0:T(8,128)}, f32[384,512]{1,0:T(8,128)}, f32[384,512]{1,0:T(8,128)}) custom-call(f32[384,512]{1,0:T(8,128)S(1)} %get-tuple-element.8.refs_0_, f32[384,512]{1,0:T(8,128)S(1)} %get-tuple-element.9.refs_1_, f32[384,512]{1,0:T(8,128)S(1)} %get-tuple-element.10.refs_2_, ...), custom_call_target="tpu_custom_call" | custom-call | tf_op jit(solution)/shard_map/hand_over/pallas_call | solution.py:556

commit v5 on v4

--- a/solution.py
+++ b/solution.py
@@ -14,6 +14,11 @@
 MESH = pl.DeviceIdType.MESH
 F32 = jnp.float32
 BF16 = jnp.bfloat16
+
+
+def inverse_radius(first, count, total_rows):
+    index = first + lax.broadcasted_iota(jnp.int32, (count, 1), 0)
+    return 1.0 / (1.0 + 3.0 * (index.astype(F32) + 0.5) / total_rows)
 
 
 def kernel(
@@ -27,7 +32,8 @@
     dust_radial,
     dust_azimuth,
     coupling,
-    potential,
+    potp,
+    edges,
     density_next,
     radial_next,
     azimuth_next,
@@ -37,7 +43,7 @@
     ga,
     fld,
     kv,
-    potp,
+    prow_in,
     near,
     far_out,
     far_in,
@@ -92,11 +98,9 @@
         load(field, fld.at[n, body_rows, :], n)
         for n, field in enumerate((dust_density, dust_radial, dust_azimuth))
     ]
-    for n, j in enumerate((3, 1)):
-        load_gr[j] = load(green_radial.at[j], gr.at[j], 6 + n)
-    load_ga = load(green_azimuth, ga, 9)
-    load_gr[2] = load(green_radial.at[2], gr.at[2], 8)
-    load_k = load(coupling, kv, 10)
+    load_inner = load(green_radial.at[pl.ds(1, 3)], gr.at[pl.ds(1, 3)], 6)
+    load_ga = load(green_azimuth, ga, 7)
+    load_k = load(coupling, kv, 8)
 
     barrier = pltpu.get_barrier_semaphore()
     for s in side + side_two:
@@ -131,27 +135,25 @@
             remote(
                 gas.at[:, cols],
                 ext.at[pl.ds(0, rows), cols],
-                gas_send.at[0, n],
+                gas_send.at[0],
                 gas_recv.at[0, n],
                 up,
             ),
             remote(
                 gas.at[:, cols],
                 ext.at[pl.ds(2 * rows, rows), cols],
-                gas_send.at[1, n],
+                gas_send.at[1],
                 gas_recv.at[1, n],
                 down,
             ),
         )
 
+    def both(up_step, down_step):
+        pl.when(has_up)(up_step)
+        pl.when(has_down)(down_step)
+
     def start_both(copies):
-        @pl.when(has_up)
-        def _():
-            copies[0].start()
-
-        @pl.when(has_down)
-        def _():
-            copies[1].start()
+        both(copies[0].start, copies[1].start)
 
     def wait_both(copies):
         @pl.when(has_up)
@@ -194,15 +196,7 @@
         pl.when(jnp.logical_and(has_down, jnp.logical_not(seam_down)))(down_step)
 
     def arrive(copies):
-        def from_up():
-            copies[0].wait_send()
-            copies[1].wait_recv()
-
-        def from_down():
-            copies[1].wait_send()
-            copies[0].wait_recv()
-
-        return from_up, from_down
+        return copies[1].wait_recv, copies[0].wait_recv
 
     def leave(copies):
         return copies[0].start, copies[1].start
@@ -221,8 +215,8 @@
         remote(fld.at[:, bottom, :], fld.at[:, halo_high, :], row_send.at[1], row_recv.at[1], down),
     )
     prow = (
-        remote(potp.at[top, :], potp.at[halo_low, :], row_send.at[2], row_recv.at[2], up),
-        remote(potp.at[bottom, :], potp.at[halo_high, :], row_send.at[3], row_recv.at[3], down),
+        remote(potp.at[top, :], prow_in.at[0], row_send.at[2], row_recv.at[2], up),
+        remote(potp.at[bottom, :], prow_in.at[1], row_send.at[3], row_recv.at[3], down),
     )
 
     @pl.when(jnp.logical_not(has_down))
@@ -230,21 +224,21 @@
         ext[0:rows, :] = jnp.zeros((rows, arc), BF16)
         gz[:, 0:rows, :] = jnp.zeros((2, rows, lead), BF16)
         fld[:, 0:8, :] = jnp.zeros((3, 8, arc), F32)
-        potp[0:8, :] = jnp.zeros((8, arc), F32)
+        prow_in[0] = jnp.zeros((8, arc), F32)
 
     @pl.when(jnp.logical_not(has_up))
     def _():
         ext[2 * rows : 3 * rows, :] = jnp.zeros((rows, arc), BF16)
         gz[:, 2 * rows : 3 * rows, :] = jnp.zeros((2, rows, lead), BF16)
         fld[:, rows + 8 : rows + 16, :] = jnp.zeros((3, 8, arc), F32)
-        potp[rows + 8 : rows + 16, :] = jnp.zeros((8, arc), F32)
+        prow_in[1] = jnp.zeros((8, arc), F32)
 
     def col_copy(kind, d):
         where = side_two[d] if kind == 2 else side[d]
         return remote(
             col_out.at[kind, d],
             col_in.at[kind, d],
-            col_send.at[kind, d],
+            col_send.at[d],
             col_recv.at[kind, d],
             {"sector": where},
         )
@@ -258,7 +252,6 @@
 
     for copy in load_fields:
         copy.wait()
-    start_both(drow)
     for d in range(2):
         for n in range(3):
             col_out[0, d, n : n + 1, :] = edge(fld[n, 8 : 8 + rows, edge_tile(d)], d)
@@ -272,7 +265,7 @@
         return remote(
             far_out.at[d, part, cols],
             far_in.at[d, part, cols],
-            far_send.at[d, n],
+            far_send.at[d],
             far_recv.at[d, n],
             {"sector": side[d]},
         )
@@ -290,8 +283,8 @@
         return remote(
             part_out.at[d, part, :],
             part_in.at[d, part, :],
-            part_send.at[d, c],
-            part_recv.at[d, c],
+            part_send.at[d],
+            part_recv.at[d, min(c, chunks)],
             {"sector": side[d]},
         )
 
@@ -311,7 +304,7 @@
         on_seam(first_seam(d, 2).start, first_seam(d, 0).start)
 
     for n in range(whole):
-        wait_both(gas_copies(n))
+        both(*arrive(gas_copies(n)))
         cols = slice(pieces[n][0], pieces[n][0] + pieces[n][1])
         for d, j in ((0, 4), (1, 0)):
             far_out[d, :, cols] = jnp.dot(
@@ -319,7 +312,7 @@
             ).astype(BF16)
             far_copy(d, n).start()
     pl.when(jnp.logical_not(early))(pass_on)
-    wait_both(gas_copies(whole))
+    both(*arrive(gas_copies(whole)))
     last = slice(pieces[whole][0], pieces[whole][0] + pieces[whole][1])
     for c in order:
         part = slice(c * chunk, (c + 1) * chunk)
@@ -329,9 +322,9 @@
             ).astype(BF16)
             far_copy(d, whole + c).start()
 
+    start_both(drow)
     off_seam(*arrive(gas_copies(whole + 1)))
-    load_gr[3].wait()
-    load_gr[1].wait()
+    load_inner.wait()
     load_ga.wait()
     for d, j in ((0, 3), (1, 1)):
         near[d] = jnp.dot(gr[j], ext[...], preferred_element_type=F32).astype(BF16)
@@ -371,16 +364,15 @@
         col_copy(2, d).start()
         col_own[1 - d, 0:1, :] = edge(part_out[d, :, edge_tile(1 - d)].astype(F32), 1 - d)
 
-    load_gr[2].wait()
     middle = jnp.dot(gr[2], ext[...], preferred_element_type=F32).astype(BF16)
-    potential[...] = jnp.dot(middle, ga[2], preferred_element_type=F32)
-    for d in range(2):
-        col_out[1, d, 0:1, :] = edge(potential[:, edge_tile(d)], d)
+    potp[body_rows, :] = jnp.dot(middle, ga[2], preferred_element_type=F32)
+    for d in range(2):
+        col_out[1, d, 0:1, :] = edge(potp[8 : 8 + rows, edge_tile(d)], d)
         col_copy(1, d).start()
 
     load_k.wait()
     for d in range(2):
-        col_copy(0, d).wait()
+        col_copy(0, d).wait_recv()
     wait_both(drow)
 
     def columns(block):
@@ -388,12 +380,6 @@
 
     for d in range(2):
         dcol[d] = columns(col_in[0, d])
-
-    total_rows = rows * bands
-
-    def inverse_radius(first, count):
-        index = first + lax.broadcasted_iota(jnp.int32, (count, 1), 0)
-        return 1.0 / (1.0 + 3.0 * (index.astype(F32) + 0.5) / total_rows)
 
     def dust(start, stop):
         lanes = lax.broadcasted_iota(jnp.int32, (strip, arc), 1)
@@ -405,7 +391,7 @@
             first = pl.multiple_of(step * strip, strip)
             part = pl.ds(first, strip)
             window = pl.ds(first, strip + 16)
-            inv = inverse_radius(band * rows + first, strip)
+            inv = inverse_radius(band * rows + first, strip, rows * bands)
             west_edge = dcol[0, part, :]
             east_edge = dcol[1, part, :]
             centre, above, below, east, west = [], [], [], [], []
@@ -445,16 +431,20 @@
 
     def settle(low, count):
         part = slice(low, low + count)
-        total = potential[part, :] + (
+        here = slice(8 + low, 8 + low + count)
+        potp[here, :] = potp[here, :] + (
             part_in[0, part, :].astype(F32) + part_in[1, part, :].astype(F32)
         )
-        potential[part, :] = total
-        potp[8 + low : 8 + low + count, :] = total
-        return total
-
-    for d in range(2):
-        part_copy(d, chunks).wait_recv()
-        part_copy(d, chunks + 1).wait_recv()
+
+    for d in range(2):
+        both_rims = pl.ds(0, 2 * rim)
+        remote(
+            part_out.at[d, both_rims, :],
+            part_in.at[d, both_rims, :],
+            part_send.at[d],
+            part_recv.at[d, chunks],
+            {"sector": side[d]},
+        ).wait_recv()
     settle(0, rim)
     settle(rows - rim, rim)
     start_both(prow)
@@ -462,45 +452,88 @@
     dust(0, rows)
 
     for d in range(2):
-        col_copy(1, d).wait()
-        col_copy(2, d).wait()
+        col_copy(1, d).wait_recv()
+        col_copy(2, d).wait_recv()
         row = col_in[1, d, 0:1, :] + (col_in[2, d, 0:1, :] + col_own[d, 0:1, :])
-        dcol[d] = jnp.transpose(jnp.concatenate([row, jnp.zeros((127, rows), F32)], axis=0))
-
+        edges[d] = jnp.transpose(jnp.concatenate([row, jnp.zeros((127, rows), F32)], axis=0))
+
+    for c in order:
+        for d in range(2):
+            part_copy(d, c).wait_recv()
+        settle(*span(c))
+    wait_both(prow)
+    potp[0:8, :] = prow_in[0]
+    potp[rows + 8 : rows + 16, :] = prow_in[1]
+
+    sent_cols = pl.ds(lead, arc - lead)
+    for d in range(2):
+        where = {"sector": side[d]}
+        remote(
+            far_out.at[d, :, sent_cols],
+            far_in.at[d, :, sent_cols],
+            far_send.at[d],
+            far_recv.at[d, 0],
+            where,
+        ).wait_send()
+        remote(
+            part_out.at[d], part_in.at[d], part_send.at[d], part_recv.at[d, 0], where
+        ).wait_send()
+        remote(
+            col_out.at[:, d], col_in.at[:, d], col_send.at[d], col_recv.at[0, d], where
+        ).wait_send()
+    both(
+        remote(gas, ext.at[thirds[0], :], gas_send.at[0], gas_recv.at[0, 0], up).wait_send,
+        remote(gas, ext.at[thirds[2], :], gas_send.at[1], gas_recv.at[1, 0], down).wait_send,
+    )
+
+
+def finish(
+    chunk,
+    potp,
+    edges,
+    density_part,
+    radial_part,
+    azimuth_part,
+    potential,
+    density_next,
+    radial_next,
+    azimuth_next,
+    radial,
+    azimuth,
+    sem,
+):
+    rows, arc = density_part.shape
+    band = lax.axis_index("band")
+    total_rows = rows * lax.axis_size("band")
+    copies = [
+        pltpu.make_async_copy(density_part, density_next, sem.at[0]),
+        pltpu.make_async_copy(potp.at[pl.ds(8, rows), :], potential, sem.at[1]),
+    ]
+    for copy in copies:
+        copy.start()
     lanes = lax.broadcasted_iota(jnp.int32, (chunk, arc), 1)
     is_first = lanes == 0
     is_last = lanes == arc - 1
-    for c in order:
+    for c in range(rows // chunk):
         part = slice(c * chunk, (c + 1) * chunk)
-        for d in range(2):
-            part_copy(d, c).wait_recv()
-        settle(*span(c))
-        total = potential[part, :]
-        inv = inverse_radius(band * rows + c * chunk, chunk)
-        east = jnp.where(is_last, dcol[1, part, 0:1], pltpu.roll(total, arc - 1, 1))
-        west = jnp.where(is_first, dcol[0, part, 0:1], pltpu.roll(total, 1, 1))
-        azimuth_next[part, :] = azimuth_next[part, :] - 0.5 * gravity * inv * (east - west)
-
-    wait_both(prow)
-    for c in order:
-        part = slice(c * chunk, (c + 1) * chunk)
+        cut = pl.ds(c * chunk, chunk)
         q = potp[c * chunk : (c + 1) * chunk + 16, :]
-        radial_next[part, :] = radial_next[part, :] - 0.5 * gravity * (
+        radial[part, :] = radial_part[part, :] - 0.5 * gravity * (
             q[9 : 9 + chunk] - q[7 : 7 + chunk]
         )
-    for d in range(2):
-        for n in range(whole + chunks):
-            far_copy(d, n).wait_send()
-        for c in range(chunks + 2):
-            part_copy(d, c).wait_send()
-
-
-def hand_over(*refs):
-    copies = [
-        pltpu.make_async_copy(refs[n], refs[4 + n], refs[8].at[n]) for n in range(4)
-    ]
-    for copy in copies:
-        copy.start()
+        copies.append(
+            pltpu.make_async_copy(radial.at[cut, :], radial_next.at[cut, :], sem.at[2 + 2 * c])
+        )
+        copies[-1].start()
+        mid = q[8 : 8 + chunk]
+        inv = inverse_radius(band * rows + c * chunk, chunk, total_rows)
+        east = jnp.where(is_last, edges[1, part, 0:1], pltpu.roll(mid, arc - 1, 1))
+        west = jnp.where(is_first, edges[0, part, 0:1], pltpu.roll(mid, 1, 1))
+        azimuth[part, :] = azimuth_part[part, :] - 0.5 * gravity * inv * (east - west)
+        copies.append(
+            pltpu.make_async_copy(azimuth.at[cut, :], azimuth_next.at[cut, :], sem.at[3 + 2 * c])
+        )
+        copies[-1].start()
     for copy in copies:
         copy.wait()
 
@@ -514,9 +547,13 @@
     operands = (gas, green_radial, green_azimuth, rho, u, w, coupling)
     results = pl.pallas_call(
         functools.partial(kernel, chunk, strip, pieces),
-        out_shape=[pltpu.VMEM((rows, arc), F32)] * 4,
+        out_shape=[
+            pltpu.VMEM((rows + 16, arc), F32),
+            pltpu.VMEM((2, rows, 128), F32),
+        ]
+        + [pltpu.VMEM((rows, arc), F32)] * 3,
         in_specs=[pl.BlockSpec(memory_space=pltpu.HBM)] * 7,
-        out_specs=[pl.BlockSpec(memory_space=pltpu.VMEM)] * 4,
+        out_specs=[pl.BlockSpec(memory_space=pltpu.VMEM)] * 5,
         scratch_shapes=[
             pltpu.VMEM((3 * rows, arc), BF16),
             pltpu.VMEM((2, 3 * rows, lead), BF16),
@@ -524,7 +561,7 @@
             pltpu.VMEM((5, arc, arc), BF16),
             pltpu.VMEM((3, rows + 16, arc), F32),
             pltpu.VMEM((rows, arc), BF16),
-            pltpu.VMEM((rows + 16, arc), F32),
+            pltpu.VMEM((2, 8, arc), F32),
             pltpu.VMEM((2, rows, arc), BF16),
             pltpu.VMEM((2, rows, arc), BF16),
             pltpu.VMEM((2, rows, arc), BF16),
@@ -534,19 +571,19 @@
             pltpu.VMEM((3, 2, 8, rows), F32),
             pltpu.VMEM((2, 8, rows), F32),
             pltpu.VMEM((2, rows, 128), F32),
-            dma((11,)),
-            dma((2, steps)),
+            dma((9,)),
+            dma((2,)),
             dma((2, steps)),
             dma((2, 3)),
             dma((2, 3)),
             dma((4,)),
             dma((4,)),
+            dma((2,)),
             dma((3, 2)),
-            dma((3, 2)),
+            dma((2,)),
             dma((2, steps - 2 + chunks)),
-            dma((2, steps - 2 + chunks)),
-            dma((2, chunks + 2)),
-            dma((2, chunks + 2)),
+            dma((2,)),
+            dma((2, chunks + 1)),
         ],
         compiler_params=pltpu.CompilerParams(
             collective_id=0, has_side_effects=True, vmem_limit_bytes=50 * 2**20
@@ -554,13 +591,17 @@
         name="disc",
     )(*[pltpu.with_memory_space_constraint(x, pltpu.HBM) for x in operands])
     return pl.pallas_call(
-        hand_over,
+        functools.partial(finish, chunk),
         out_shape=[jax.ShapeDtypeStruct((rows, arc), F32)] * 4,
-        in_specs=[pl.BlockSpec(memory_space=pltpu.VMEM)] * 4,
+        in_specs=[pl.BlockSpec(memory_space=pltpu.VMEM)] * 5,
         out_specs=[pl.BlockSpec(memory_space=pl.ANY)] * 4,
-        scratch_shapes=[dma((4,))],
-        compiler_params=pltpu.CompilerParams(vmem_limit_bytes=2**20),
-        name="hand_over",
+        scratch_shapes=[
+            pltpu.VMEM((rows, arc), F32),
+            pltpu.VMEM((rows, arc), F32),
+            dma((2 + 2 * chunks,)),
+        ],
+        compiler_params=pltpu.CompilerParams(vmem_limit_bytes=4 * 2**20),
+        name="finish",
     )(*[pltpu.with_memory_space_constraint(r, pltpu.VMEM) for r in results])
 
 

time: 38 us -> 37.2 us (0.979)
  Pallas kernels: 37.3 us -> 36.5 us
    pallas_call x1, Pallas kernels: 35.6 us -> 34.8 us  [body(): pl.pallas_call(functools.partial(kernel, chunk, strip, pieces), out_shape...]
where the time goes in v5:
time: 37.2 us
  Pallas kernels  36.5 us (98%)
  between operations  0.64 us (2%)
    pallas_call x1, Pallas kernels, body(): pl.pallas_call(functools.partial(kernel, chunk, strip, pieces), out_shape...  34.8 us
    pallas_call x1, Pallas kernels, body(): pl.pallas_call(functools.partial(finish, chunk), out_shape=[jax.ShapeDtyp...  1.74 us

profile of v5, /device:TPU:7, one launch (start us, length us, event | category | flops | bytes accessed | tf_op | source)
XLA Modules:
  0.0 37.2 jit_solution(13326450348292982173)
XLA Ops:
  0.6 34.8 %disc.1 = (f32[400,512]{1,0:T(8,128)S(1)}, f32[2,384,128]{2,1,0:T(8,128)S(1)}, f32[384,512]{1,0:T(8,128)S(1)}, f32[384,512]{1,0:T(8,128)S(1)}, f32[384,512]{1,0:T(8,128)S(1)}) custom-call(bf16[384,512]{1,0:T(8,128)(2,1)} %gas.1, bf16[5,384,1152]{2,1,0:T(8,128)(2,1)} %green_radial.1, bf16[5,512,512]{2,1,0:T(8,128)(2,1)} %green_azimuth.1, ...), custom_call_target="tpu_custom_call" | custom-call | tf_op jit(solution)/shard_map/disc/pallas_call | solution.py:548
  35.4 1.7 %finish.1 = (f32[384,512]{1,0:T(8,128)}, f32[384,512]{1,0:T(8,128)}, f32[384,512]{1,0:T(8,128)}, f32[384,512]{1,0:T(8,128)}) custom-call(f32[400,512]{1,0:T(8,128)S(1)} %get-tuple-element.9.potp, f32[2,384,128]{2,1,0:T(8,128)S(1)} %get-tuple-element.10.edges, f32[384,512]{1,0:T(8,128)S(1)} %get-tuple-element.11.density_part, ...), custom_call_target="tpu_custom_call" | custom-call | tf_op jit(solution)/shard_map/finish/pallas_call | solution.py:593

commit v6 on v5

--- a/solution.py
+++ b/solution.py
@@ -39,6 +39,7 @@
     azimuth_next,
     ext,
     gz,
+    hop,
     gr,
     ga,
     fld,
@@ -58,6 +59,7 @@
     gas_recv,
     first_send,
     first_recv,
+    hop_sem,
     row_send,
     row_recv,
     col_send,
@@ -79,6 +81,8 @@
     has_down = band > 0
     seam_up = band == bands // 2 - 1
     seam_down = band == bands // 2
+    seam = jnp.logical_or(seam_up, seam_down)
+    end = jnp.logical_or(band == 0, band == bands - 1)
 
     lead = gz.shape[2]
     whole = len(pieces) - 2
@@ -114,7 +118,24 @@
     def _():
         pl.semaphore_signal(barrier, inc=1, device_id={"band": band - 1}, device_id_type=MESH)
 
-    pl.semaphore_wait(barrier, 4 + has_up.astype(jnp.int32) + has_down.astype(jnp.int32))
+    @pl.when(seam)
+    def _():
+        for b in (0, bands - 1):
+            pl.semaphore_signal(barrier, inc=1, device_id={"band": b}, device_id_type=MESH)
+
+    @pl.when(end)
+    def _():
+        for b in (bands // 2 - 1, bands // 2):
+            pl.semaphore_signal(barrier, inc=1, device_id={"band": b}, device_id_type=MESH)
+
+    pl.semaphore_wait(
+        barrier,
+        4
+        + has_up.astype(jnp.int32)
+        + has_down.astype(jnp.int32)
+        + 2 * seam.astype(jnp.int32)
+        + 2 * end.astype(jnp.int32),
+    )
 
     def remote(src, dst, send, recv, where):
         return pltpu.make_async_remote_copy(
@@ -129,8 +150,8 @@
     up = {"band": band + 1}
     down = {"band": band - 1}
 
-    def gas_copies(n):
-        cols = pl.ds(*pieces[n])
+    def gas_copies(n, part=None):
+        cols = pl.ds(*(part or pieces[n]))
         return (
             remote(
                 gas.at[:, cols],
@@ -201,9 +222,30 @@
     def leave(copies):
         return copies[0].start, copies[1].start
 
+    first_col, count = pieces[whole]
+    straight = (first_col, count // 2)
+    around = pl.ds(first_col + count // 2, count // 2)
+    out_up = remote(
+        gas.at[:, around], hop, gas_send.at[0], hop_sem.at[0], {"band": bands - 1}
+    )
+    out_down = remote(gas.at[:, around], hop, gas_send.at[1], hop_sem.at[0], {"band": 0})
+    on_up = remote(
+        hop, ext.at[pl.ds(0, rows), around], hop_sem.at[1], hop_sem.at[2], {"band": bands // 2}
+    )
+    on_down = remote(
+        hop,
+        ext.at[pl.ds(2 * rows, rows), around],
+        hop_sem.at[1],
+        hop_sem.at[2],
+        {"band": bands // 2 - 1},
+    )
+
     on_seam(*leave(gas_copies(whole + 1)))
-    for n in range(whole + 1):
+    on_seam(out_up.start, out_down.start)
+    for n in range(whole):
         start_both(gas_copies(n))
+    on_seam(*leave(gas_copies(whole, straight)))
+    off_seam(*leave(gas_copies(whole)))
     off_seam(*leave(gas_copies(whole + 1)))
 
     top = pl.ds(rows, 8)
@@ -312,7 +354,19 @@
             ).astype(BF16)
             far_copy(d, n).start()
     pl.when(jnp.logical_not(early))(pass_on)
-    both(*arrive(gas_copies(whole)))
+    @pl.when(band == bands - 1)
+    def _():
+        out_up.wait_recv()
+        on_up.start()
+
+    @pl.when(band == 0)
+    def _():
+        out_down.wait_recv()
+        on_down.start()
+
+    off_seam(*arrive(gas_copies(whole)))
+    on_seam(*arrive(gas_copies(whole, straight)))
+    on_seam(on_down.wait_recv, on_up.wait_recv)
     last = slice(pieces[whole][0], pieces[whole][0] + pieces[whole][1])
     for c in order:
         part = slice(c * chunk, (c + 1) * chunk)
@@ -465,6 +519,8 @@
     potp[0:8, :] = prow_in[0]
     potp[rows + 8 : rows + 16, :] = prow_in[1]
 
+    pl.when(band == bands - 1)(on_up.wait_send)
+    pl.when(band == 0)(on_down.wait_send)
     sent_cols = pl.ds(lead, arc - lead)
     for d in range(2):
         where = {"sector": side[d]}
@@ -557,6 +613,7 @@
         scratch_shapes=[
             pltpu.VMEM((3 * rows, arc), BF16),
             pltpu.VMEM((2, 3 * rows, lead), BF16),
+            pltpu.VMEM((rows, pieces[-2][1] // 2), BF16),
             pltpu.VMEM((5, rows, 3 * rows), BF16),
             pltpu.VMEM((5, arc, arc), BF16),
             pltpu.VMEM((3, rows + 16, arc), F32),
@@ -576,6 +633,7 @@
             dma((2, steps)),
             dma((2, 3)),
             dma((2, 3)),
+            dma((3,)),
             dma((4,)),
             dma((4,)),
             dma((2,)),

time: 37.2 us -> 36.4 us (0.978)
  Pallas kernels: 36.5 us -> 35.7 us
    pallas_call x1, Pallas kernels: 34.8 us -> 33.9 us  [body(): pl.pallas_call(functools.partial(kernel, chunk, strip, pieces), out_shape...]
where the time goes in v6:
time: 36.4 us; the launch traced here: 36.3 us
  Pallas kernels  35.7 us (98%)
  between operations  0.64 us (2%)
    pallas_call x1, Pallas kernels, body(): pl.pallas_call(functools.partial(kernel, chunk, strip, pieces), out_shape...  33.9 us
    pallas_call x1, Pallas kernels, body(): pl.pallas_call(functools.partial(finish, chunk), out_shape=[jax.ShapeDtyp...  1.74 us

profile of v6, /device:TPU:7, one launch (start us, length us, event | category | flops | bytes accessed | tf_op | source)
XLA Modules:
  0.0 36.3 jit_solution(3650221544409075558)
XLA Ops:
  0.6 33.9 %disc.1 = (f32[400,512]{1,0:T(8,128)S(1)}, f32[2,384,128]{2,1,0:T(8,128)S(1)}, f32[384,512]{1,0:T(8,128)S(1)}, f32[384,512]{1,0:T(8,128)S(1)}, f32[384,512]{1,0:T(8,128)S(1)}) custom-call(bf16[384,512]{1,0:T(8,128)(2,1)} %gas.1, bf16[5,384,1152]{2,1,0:T(8,128)(2,1)} %green_radial.1, bf16[5,512,512]{2,1,0:T(8,128)(2,1)} %green_azimuth.1, ...), custom_call_target="tpu_custom_call" | custom-call | tf_op jit(solution)/shard_map/disc/pallas_call | solution.py:604
  34.6 1.7 %finish.1 = (f32[384,512]{1,0:T(8,128)}, f32[384,512]{1,0:T(8,128)}, f32[384,512]{1,0:T(8,128)}, f32[384,512]{1,0:T(8,128)}) custom-call(f32[400,512]{1,0:T(8,128)S(1)} %get-tuple-element.9.potp, f32[2,384,128]{2,1,0:T(8,128)S(1)} %get-tuple-element.10.edges, f32[384,512]{1,0:T(8,128)S(1)} %get-tuple-element.11.density_part, ...), custom_call_target="tpu_custom_call" | custom-call | tf_op jit(solution)/shard_map/finish/pallas_call | solution.py:651

commit v7 on v6

--- a/solution.py
+++ b/solution.py
@@ -32,7 +32,9 @@
     dust_radial,
     dust_azimuth,
     coupling,
-    potp,
+    mid_pot,
+    part_in,
+    rims,
     edges,
     density_next,
     radial_next,
@@ -44,12 +46,12 @@
     ga,
     fld,
     kv,
+    prow_out,
     prow_in,
     near,
     far_out,
     far_in,
     part_out,
-    part_in,
     col_out,
     col_in,
     col_own,
@@ -87,6 +89,28 @@
     lead = gz.shape[2]
     whole = len(pieces) - 2
 
+    barrier = pltpu.get_barrier_semaphore()
+    for s in side + side_two:
+        pl.semaphore_signal(barrier, inc=1, device_id={"sector": s}, device_id_type=MESH)
+
+    @pl.when(has_up)
+    def _():
+        pl.semaphore_signal(barrier, inc=1, device_id={"band": band + 1}, device_id_type=MESH)
+
+    @pl.when(has_down)
+    def _():
+        pl.semaphore_signal(barrier, inc=1, device_id={"band": band - 1}, device_id_type=MESH)
+
+    @pl.when(seam)
+    def _():
+        for b in (0, bands - 1):
+            pl.semaphore_signal(barrier, inc=1, device_id={"band": b}, device_id_type=MESH)
+
+    @pl.when(end)
+    def _():
+        for b in (bands // 2 - 1, bands // 2):
+            pl.semaphore_signal(barrier, inc=1, device_id={"band": b}, device_id_type=MESH)
+
     def load(src, dst, n):
         copy = pltpu.make_async_copy(src, dst, load_sem.at[n])
         copy.start()
@@ -106,28 +130,7 @@
     load_ga = load(green_azimuth, ga, 7)
     load_k = load(coupling, kv, 8)
 
-    barrier = pltpu.get_barrier_semaphore()
-    for s in side + side_two:
-        pl.semaphore_signal(barrier, inc=1, device_id={"sector": s}, device_id_type=MESH)
-
-    @pl.when(has_up)
-    def _():
-        pl.semaphore_signal(barrier, inc=1, device_id={"band": band + 1}, device_id_type=MESH)
-
-    @pl.when(has_down)
-    def _():
-        pl.semaphore_signal(barrier, inc=1, device_id={"band": band - 1}, device_id_type=MESH)
-
-    @pl.when(seam)
-    def _():
-        for b in (0, bands - 1):
-            pl.semaphore_signal(barrier, inc=1, device_id={"band": b}, device_id_type=MESH)
-
-    @pl.when(end)
-    def _():
-        for b in (bands // 2 - 1, bands // 2):
-            pl.semaphore_signal(barrier, inc=1, device_id={"band": b}, device_id_type=MESH)
-
+    load_gas.wait()
     pl.semaphore_wait(
         barrier,
         4
@@ -154,14 +157,14 @@
         cols = pl.ds(*(part or pieces[n]))
         return (
             remote(
-                gas.at[:, cols],
+                ext.at[own, cols],
                 ext.at[pl.ds(0, rows), cols],
                 gas_send.at[0],
                 gas_recv.at[0, n],
                 up,
             ),
             remote(
-                gas.at[:, cols],
+                ext.at[own, cols],
                 ext.at[pl.ds(2 * rows, rows), cols],
                 gas_send.at[1],
                 gas_recv.at[1, n],
@@ -197,7 +200,7 @@
     head = pl.ds(0, lead)
 
     def first_own(d):
-        return first_copy(d, 1, gas.at[:, head], {"sector": side[d]}, 1)
+        return first_copy(d, 1, ext.at[own, head], {"sector": side[d]}, 1)
 
     def first_on(d, third):
         where = up if third == 0 else down
@@ -206,8 +209,6 @@
     def first_seam(d, third):
         return first_copy(d, third, ext.at[thirds[third], head], {"sector": side[d]}, 2 - third)
 
-    for d in range(2):
-        first_own(d).start()
     def on_seam(up_step, down_step):
         pl.when(seam_up)(up_step)
         pl.when(seam_down)(down_step)
@@ -226,9 +227,9 @@
     straight = (first_col, count // 2)
     around = pl.ds(first_col + count // 2, count // 2)
     out_up = remote(
-        gas.at[:, around], hop, gas_send.at[0], hop_sem.at[0], {"band": bands - 1}
-    )
-    out_down = remote(gas.at[:, around], hop, gas_send.at[1], hop_sem.at[0], {"band": 0})
+        ext.at[own, around], hop, gas_send.at[0], hop_sem.at[0], {"band": bands - 1}
+    )
+    out_down = remote(ext.at[own, around], hop, gas_send.at[1], hop_sem.at[0], {"band": 0})
     on_up = remote(
         hop, ext.at[pl.ds(0, rows), around], hop_sem.at[1], hop_sem.at[2], {"band": bands // 2}
     )
@@ -244,6 +245,8 @@
     on_seam(out_up.start, out_down.start)
     for n in range(whole):
         start_both(gas_copies(n))
+    for d in range(2):
+        first_own(d).start()
     on_seam(*leave(gas_copies(whole, straight)))
     off_seam(*leave(gas_copies(whole)))
     off_seam(*leave(gas_copies(whole + 1)))
@@ -257,8 +260,8 @@
         remote(fld.at[:, bottom, :], fld.at[:, halo_high, :], row_send.at[1], row_recv.at[1], down),
     )
     prow = (
-        remote(potp.at[top, :], prow_in.at[0], row_send.at[2], row_recv.at[2], up),
-        remote(potp.at[bottom, :], prow_in.at[1], row_send.at[3], row_recv.at[3], down),
+        remote(prow_out.at[0], prow_in.at[0], row_send.at[2], row_recv.at[2], up),
+        remote(prow_out.at[1], prow_in.at[1], row_send.at[3], row_recv.at[3], down),
     )
 
     @pl.when(jnp.logical_not(has_down))
@@ -331,7 +334,6 @@
         )
 
     order = [(chunks - n) % chunks for n in range(chunks)]
-    load_gas.wait()
     load_gr[4].wait()
     load_gr[0].wait()
     def pass_on():
@@ -419,9 +421,9 @@
         col_own[1 - d, 0:1, :] = edge(part_out[d, :, edge_tile(1 - d)].astype(F32), 1 - d)
 
     middle = jnp.dot(gr[2], ext[...], preferred_element_type=F32).astype(BF16)
-    potp[body_rows, :] = jnp.dot(middle, ga[2], preferred_element_type=F32)
-    for d in range(2):
-        col_out[1, d, 0:1, :] = edge(potp[8 : 8 + rows, edge_tile(d)], d)
+    mid_pot[...] = jnp.dot(middle, ga[2], preferred_element_type=F32)
+    for d in range(2):
+        col_out[1, d, 0:1, :] = edge(mid_pot[:, edge_tile(d)], d)
         col_copy(1, d).start()
 
     load_k.wait()
@@ -483,10 +485,9 @@
                 + diffusion * lap[2]
             )
 
-    def settle(low, count):
-        part = slice(low, low + count)
-        here = slice(8 + low, 8 + low + count)
-        potp[here, :] = potp[here, :] + (
+    def settled(low):
+        part = slice(low, low + rim)
+        return mid_pot[part, :] + (
             part_in[0, part, :].astype(F32) + part_in[1, part, :].astype(F32)
         )
 
@@ -499,8 +500,8 @@
             part_recv.at[d, chunks],
             {"sector": side[d]},
         ).wait_recv()
-    settle(0, rim)
-    settle(rows - rim, rim)
+    prow_out[1] = settled(0)[0:8]
+    prow_out[0] = settled(rows - rim)[rim - 8 : rim]
     start_both(prow)
 
     dust(0, rows)
@@ -514,10 +515,8 @@
     for c in order:
         for d in range(2):
             part_copy(d, c).wait_recv()
-        settle(*span(c))
     wait_both(prow)
-    potp[0:8, :] = prow_in[0]
-    potp[rows + 8 : rows + 16, :] = prow_in[1]
+    rims[...] = prow_in[...]
 
     pl.when(band == bands - 1)(on_up.wait_send)
     pl.when(band == 0)(on_down.wait_send)
@@ -538,14 +537,16 @@
             col_out.at[:, d], col_in.at[:, d], col_send.at[d], col_recv.at[0, d], where
         ).wait_send()
     both(
-        remote(gas, ext.at[thirds[0], :], gas_send.at[0], gas_recv.at[0, 0], up).wait_send,
-        remote(gas, ext.at[thirds[2], :], gas_send.at[1], gas_recv.at[1, 0], down).wait_send,
+        remote(ext.at[own, :], ext.at[thirds[0], :], gas_send.at[0], gas_recv.at[0, 0], up).wait_send,
+        remote(ext.at[own, :], ext.at[thirds[2], :], gas_send.at[1], gas_recv.at[1, 0], down).wait_send,
     )
 
 
 def finish(
     chunk,
-    potp,
+    mid_pot,
+    parts,
+    rims,
     edges,
     density_part,
     radial_part,
@@ -554,6 +555,7 @@
     density_next,
     radial_next,
     azimuth_next,
+    potp,
     radial,
     azimuth,
     sem,
@@ -561,16 +563,28 @@
     rows, arc = density_part.shape
     band = lax.axis_index("band")
     total_rows = rows * lax.axis_size("band")
-    copies = [
-        pltpu.make_async_copy(density_part, density_next, sem.at[0]),
-        pltpu.make_async_copy(potp.at[pl.ds(8, rows), :], potential, sem.at[1]),
-    ]
-    for copy in copies:
-        copy.start()
+    chunks = rows // chunk
+    copies = [pltpu.make_async_copy(density_part, density_next, sem.at[0])]
+    copies[0].start()
+    potp[0:8, :] = rims[0]
+    potp[rows + 8 : rows + 16, :] = rims[1]
+    for c in range(chunks):
+        part = slice(c * chunk, (c + 1) * chunk)
+        potp[8 + c * chunk : 8 + (c + 1) * chunk, :] = mid_pot[part, :] + (
+            parts[0, part, :].astype(F32) + parts[1, part, :].astype(F32)
+        )
+        copies.append(
+            pltpu.make_async_copy(
+                potp.at[pl.ds(8 + c * chunk, chunk), :],
+                potential.at[pl.ds(c * chunk, chunk), :],
+                sem.at[1 + c],
+            )
+        )
+        copies[-1].start()
     lanes = lax.broadcasted_iota(jnp.int32, (chunk, arc), 1)
     is_first = lanes == 0
     is_last = lanes == arc - 1
-    for c in range(rows // chunk):
+    for c in range(chunks):
         part = slice(c * chunk, (c + 1) * chunk)
         cut = pl.ds(c * chunk, chunk)
         q = potp[c * chunk : (c + 1) * chunk + 16, :]
@@ -578,7 +592,7 @@
             q[9 : 9 + chunk] - q[7 : 7 + chunk]
         )
         copies.append(
-            pltpu.make_async_copy(radial.at[cut, :], radial_next.at[cut, :], sem.at[2 + 2 * c])
+            pltpu.make_async_copy(radial.at[cut, :], radial_next.at[cut, :], sem.at[1 + chunks + 2 * c])
         )
         copies[-1].start()
         mid = q[8 : 8 + chunk]
@@ -587,7 +601,7 @@
         west = jnp.where(is_first, edges[0, part, 0:1], pltpu.roll(mid, 1, 1))
         azimuth[part, :] = azimuth_part[part, :] - 0.5 * gravity * inv * (east - west)
         copies.append(
-            pltpu.make_async_copy(azimuth.at[cut, :], azimuth_next.at[cut, :], sem.at[3 + 2 * c])
+            pltpu.make_async_copy(azimuth.at[cut, :], azimuth_next.at[cut, :], sem.at[2 + chunks + 2 * c])
         )
         copies[-1].start()
     for copy in copies:
@@ -604,12 +618,14 @@
     results = pl.pallas_call(
         functools.partial(kernel, chunk, strip, pieces),
         out_shape=[
-            pltpu.VMEM((rows + 16, arc), F32),
+            pltpu.VMEM((rows, arc), F32),
+            pltpu.VMEM((2, rows, arc), BF16),
+            pltpu.VMEM((2, 8, arc), F32),
             pltpu.VMEM((2, rows, 128), F32),
         ]
         + [pltpu.VMEM((rows, arc), F32)] * 3,
         in_specs=[pl.BlockSpec(memory_space=pltpu.HBM)] * 7,
-        out_specs=[pl.BlockSpec(memory_space=pltpu.VMEM)] * 5,
+        out_specs=[pl.BlockSpec(memory_space=pltpu.VMEM)] * 7,
         scratch_shapes=[
             pltpu.VMEM((3 * rows, arc), BF16),
             pltpu.VMEM((2, 3 * rows, lead), BF16),
@@ -619,7 +635,7 @@
             pltpu.VMEM((3, rows + 16, arc), F32),
             pltpu.VMEM((rows, arc), BF16),
             pltpu.VMEM((2, 8, arc), F32),
-            pltpu.VMEM((2, rows, arc), BF16),
+            pltpu.VMEM((2, 8, arc), F32),
             pltpu.VMEM((2, rows, arc), BF16),
             pltpu.VMEM((2, rows, arc), BF16),
             pltpu.VMEM((2, rows, arc), BF16),
@@ -651,12 +667,13 @@
     return pl.pallas_call(
         functools.partial(finish, chunk),
         out_shape=[jax.ShapeDtypeStruct((rows, arc), F32)] * 4,
-        in_specs=[pl.BlockSpec(memory_space=pltpu.VMEM)] * 5,
+        in_specs=[pl.BlockSpec(memory_space=pltpu.VMEM)] * 7,
         out_specs=[pl.BlockSpec(memory_space=pl.ANY)] * 4,
         scratch_shapes=[
+            pltpu.VMEM((rows + 16, arc), F32),
             pltpu.VMEM((rows, arc), F32),
             pltpu.VMEM((rows, arc), F32),
-            dma((2 + 2 * chunks,)),
+            dma((1 + 3 * chunks,)),
         ],
         compiler_params=pltpu.CompilerParams(vmem_limit_bytes=4 * 2**20),
         name="finish",

time: 36.4 us -> 36.2 us (level)
  no operation moved by 1% of the time
where the time goes in v7:
time: 36.2 us; the launch traced here: 36.1 us
  Pallas kernels  35.5 us (98%)
  between operations  0.64 us (2%)
    pallas_call x1, Pallas kernels, body(): pl.pallas_call(functools.partial(kernel, chunk, strip, pieces), out_shape...  33.7 us
    pallas_call x1, Pallas kernels, body(): pl.pallas_call(functools.partial(finish, chunk), out_shape=[jax.ShapeDtyp...  1.76 us

profile of v7, /device:TPU:7, one launch (start us, length us, event | category | flops | bytes accessed | tf_op | source)
XLA Modules:
  0.0 36.1 jit_solution(3631154933174118087)
XLA Ops:
  0.6 33.7 %disc.1 = (f32[384,512]{1,0:T(8,128)S(1)}, bf16[2,384,512]{2,1,0:T(8,128)(2,1)S(1)}, f32[2,8,512]{2,1,0:T(8,128)S(1)}, f32[2,384,128]{2,1,0:T(8,128)S(1)}, f32[3...) custom-call(bf16[384,512]{1,0:T(8,128)(2,1)} %gas.1, bf16[5,384,1152]{2,1,0:T(8,128)(2,1)} %green_radial.1, ...), custom_call_target="tpu_custom_call" | custom-call | tf_op jit(solution)/shard_map/disc/pallas_call | solution.py:618
  34.3 1.8 %finish.1 = (f32[384,512]{1,0:T(8,128)}, f32[384,512]{1,0:T(8,128)}, f32[384,512]{1,0:T(8,128)}, f32[384,512]{1,0:T(8,128)}) custom-call(f32[384,512]{1,0:T(8,128)S(1)} %get-tuple-element.11.mid_pot, bf16[2,384,512]{2,1,0:T(8,128)(2,1)S(1)} %get-tuple-element.12.parts, f32[2,8,512]{2,1,0:T(8,128)S(1)} %get-tuple-element.13.rims, ...), custom_call_target="tpu_custom_call" | custom-call | tf_op jit(solution)/shard_map/finish/pallas_call | solution.py:667

commit v8 on v7

--- a/solution.py
+++ b/solution.py
@@ -121,12 +121,14 @@
     load_gas = load(gas, ext.at[own, :], 3)
     load_gr = {}
     for n, j in enumerate((4, 0)):
-        load_gr[j] = load(green_radial.at[j], gr.at[j], 4 + n)
+        load_gr[j] = load(green_radial.at[j], gr.at[n], 4 + n)
     load_fields = [
         load(field, fld.at[n, body_rows, :], n)
         for n, field in enumerate((dust_density, dust_radial, dust_azimuth))
     ]
-    load_inner = load(green_radial.at[pl.ds(1, 3)], gr.at[pl.ds(1, 3)], 6)
+    load_inner = [
+        load(green_radial.at[j], gr.at[n], m) for j, n, m in ((3, 2, 6), (1, 3, 9), (2, 4, 10))
+    ]
     load_ga = load(green_azimuth, ga, 7)
     load_k = load(coupling, kv, 8)
 
@@ -352,7 +354,7 @@
         cols = slice(pieces[n][0], pieces[n][0] + pieces[n][1])
         for d, j in ((0, 4), (1, 0)):
             far_out[d, :, cols] = jnp.dot(
-                gr[j], ext[:, cols], preferred_element_type=F32
+                gr[d], ext[:, cols], preferred_element_type=F32
             ).astype(BF16)
             far_copy(d, n).start()
     pl.when(jnp.logical_not(early))(pass_on)
@@ -372,18 +374,25 @@
     last = slice(pieces[whole][0], pieces[whole][0] + pieces[whole][1])
     for c in order:
         part = slice(c * chunk, (c + 1) * chunk)
-        for d, j in ((0, 4), (1, 0)):
-            far_out[d, part, last] = jnp.dot(
-                gr[j, part, :], ext[:, last], preferred_element_type=F32
-            ).astype(BF16)
+        pair = jnp.dot(
+            gr[0:2, part, :].reshape(2 * chunk, 3 * rows),
+            ext[:, last],
+            preferred_element_type=F32,
+        ).astype(BF16)
+        for d in range(2):
+            far_out[d, part, last] = pair[d * chunk : (d + 1) * chunk]
             far_copy(d, whole + c).start()
 
     start_both(drow)
     off_seam(*arrive(gas_copies(whole + 1)))
-    load_inner.wait()
+    for copy in load_inner:
+        copy.wait()
     load_ga.wait()
-    for d, j in ((0, 3), (1, 1)):
-        near[d] = jnp.dot(gr[j], ext[...], preferred_element_type=F32).astype(BF16)
+    pair = jnp.dot(
+        gr[2:4].reshape(2 * rows, 3 * rows), ext[...], preferred_element_type=F32
+    ).astype(BF16)
+    for d in range(2):
+        near[d] = pair[d * rows : (d + 1) * rows]
 
     for d, j in ((0, 4), (1, 0)):
 
@@ -397,7 +406,7 @@
             first_on(d, 2).wait_send()
             first_on(d, 0).wait_recv()
 
-        far_in[d, :, 0:lead] = jnp.dot(gr[j], gz[d], preferred_element_type=F32).astype(BF16)
+        far_in[d, :, 0:lead] = jnp.dot(gr[d], gz[d], preferred_element_type=F32).astype(BF16)
     for d in range(2):
         for n in range(whole):
             far_copy(d, n).wait_recv()
@@ -420,7 +429,7 @@
         col_copy(2, d).start()
         col_own[1 - d, 0:1, :] = edge(part_out[d, :, edge_tile(1 - d)].astype(F32), 1 - d)
 
-    middle = jnp.dot(gr[2], ext[...], preferred_element_type=F32).astype(BF16)
+    middle = jnp.dot(gr[4], ext[...], preferred_element_type=F32).astype(BF16)
     mid_pot[...] = jnp.dot(middle, ga[2], preferred_element_type=F32)
     for d in range(2):
         col_out[1, d, 0:1, :] = edge(mid_pot[:, edge_tile(d)], d)
@@ -644,7 +653,7 @@
             pltpu.VMEM((3, 2, 8, rows), F32),
             pltpu.VMEM((2, 8, rows), F32),
             pltpu.VMEM((2, rows, 128), F32),
-            dma((9,)),
+            dma((11,)),
             dma((2,)),
             dma((2, steps)),
             dma((2, 3)),

time: 36.2 us -> 35.8 us (0.989)
  Pallas kernels: 35.5 us -> 35.1 us
    pallas_call x1, Pallas kernels: 33.7 us -> 33.3 us  [body(): pl.pallas_call(functools.partial(kernel, chunk, strip, pieces), out_shape...]
where the time goes in v8:
time: 35.8 us; the launch traced here: 35.7 us
  Pallas kernels  35.1 us (98%)
  between operations  0.64 us (2%)
    pallas_call x1, Pallas kernels, body(): pl.pallas_call(functools.partial(kernel, chunk, strip, pieces), out_shape...  33.3 us
    pallas_call x1, Pallas kernels, body(): pl.pallas_call(functools.partial(finish, chunk), out_shape=[jax.ShapeDtyp...  1.76 us

profile of v8, /device:TPU:7, one launch (start us, length us, event | category | flops | bytes accessed | tf_op | source)
XLA Modules:
  0.0 35.7 jit_solution(12677815052454268211)
XLA Ops:
  0.6 33.3 %disc.1 = (f32[384,512]{1,0:T(8,128)S(1)}, bf16[2,384,512]{2,1,0:T(8,128)(2,1)S(1)}, f32[2,8,512]{2,1,0:T(8,128)S(1)}, f32[2,384,128]{2,1,0:T(8,128)S(1)}, f32[3...) custom-call(bf16[384,512]{1,0:T(8,128)(2,1)} %gas.1, bf16[5,384,1152]{2,1,0:T(8,128)(2,1)} %green_radial.1, ...), custom_call_target="tpu_custom_call" | custom-call | tf_op jit(solution)/shard_map/disc/pallas_call | solution.py:627
  34.0 1.8 %finish.1 = (f32[384,512]{1,0:T(8,128)}, f32[384,512]{1,0:T(8,128)}, f32[384,512]{1,0:T(8,128)}, f32[384,512]{1,0:T(8,128)}) custom-call(f32[384,512]{1,0:T(8,128)S(1)} %get-tuple-element.11.mid_pot, bf16[2,384,512]{2,1,0:T(8,128)(2,1)S(1)} %get-tuple-element.12.parts, f32[2,8,512]{2,1,0:T(8,128)S(1)} %get-tuple-element.13.rims, ...), custom_call_target="tpu_custom_call" | custom-call | tf_op jit(solution)/shard_map/finish/pallas_call | solution.py:676
